TPU v7x, 256 devices: a whole 4x4x8 slice. The times are simulated.
256 devices in a mesh: grp: 4 (over y), sub: 64 (over x, z, core).
Axes of the slice: x: 4, y: 4, z: 8, core: 2. Of those that a mesh axis runs over, the one named last changes fastest.
Arguments:
- coords: bfloat16 [3, 524288], P(None, ('grp', 'sub')), may hold values from -6 to 6
- rhs: bfloat16 [32, 524288], P(None, ('grp', 'sub')), may hold values from -6 to 6
- leaf_basis: bfloat16 [64, 524288], P(None, ('grp', 'sub')), may hold values from -0.375 to 0.375
- low_transfer: bfloat16 [3584, 64, 64], P(('grp', 'sub')), may hold values from -0.5 to 0.5
- low_pairs: int32 [2, 8192], P(None, ('grp', 'sub')), may hold values from 0 to 3583, as said below
- low_blocks: bfloat16 [8192, 64, 64], P(('grp', 'sub')), may hold values from -0.75 to 0.75
- upper_transfer: bfloat16 [510, 64, 64], replicated, may hold values from -0.5 to 0.5
- upper_pairs: int32 [2, 2048], P(None, ('grp', 'sub')), may hold values from 0 to 509, as said below
- upper_blocks: bfloat16 [2048, 64, 64], P(('grp', 'sub')), may hold values from -0.75 to 0.75
- near_pairs: int32 [2, 20480], P(None, ('grp', 'sub')), may hold values from 0 to 2047, as said below
- near_count: int32 [256], P(('grp', 'sub')), may hold values from 13 to 80, as said below
Outputs:
- potential: float32 [32, 524288], P(None, ('grp', 'sub'))
Inputs may be any that keep to these rules, and one draw needn't show every extreme that they name: `near_pairs`: row 0 of column k names a leaf of device k // 80; row 1 names a leaf of that device or of the devices just before and after it in tree order, in every column, used or not. `near_count`: entry d counts the leading used columns among device d's 80 columns of near_pairs; some device uses all 80. `low_pairs`: cluster i of level h of device d has number d * 14 + 2 * 8 - 2 * (8 >> h) + i. The target of column k belongs to device k // 32; its source lies on the same level, on that device or on the device just before or after it. `upper_pairs`: upper cluster i of level j has number 2 * 256 - 2 * (256 >> j) + i. Target and source of a column lie on one level below the top and differ.
All inputs are finite; a program needn't handle non-finite values.
Results may differ from a plain program's by a relative error of at most 0.0029.
Values may be sent and summed in bfloat16 or wider, within the bound.
A program may use at most 128 MiB of HBM per device.

v0:
```python
import jax
import jax.numpy as jnp
from jax import lax
from jax.sharding import PartitionSpec as P

LEAF = 256


amplitude = 0.0625
steepness = 1.7320508075688772
block_pairs = 32
highest = lax.Precision.HIGHEST


def padded(value, sides, width):
    for axis, dim in sides:
        size, length = (lax.axis_size(axis), value.shape[dim])
        up = [(i, (i + 1) % size) for i in range(size - 1)]
        down = [(j, i) for i, j in up]
        last = lax.slice_in_dim(value, length - width, length, axis=dim)
        initial = lax.slice_in_dim(value, 0, width, axis=dim)
        before = lax.ppermute(last, axis, up)
        after = lax.ppermute(initial, axis, down)
        value = jnp.concatenate([before, value, after], axis=dim)
    return value


def matern(target_xyz, source_xyz):
    diff_x = target_xyz[0][:, :, None] - source_xyz[0][:, None, :]
    diff_y = target_xyz[1][:, :, None] - source_xyz[1][:, None, :]
    diff_z = target_xyz[2][:, :, None] - source_xyz[2][:, None, :]
    scaled = steepness * jnp.sqrt(diff_x * diff_x + diff_y * diff_y + diff_z * diff_z)
    return (amplitude * (1.0 + scaled) * jnp.exp(-scaled)).astype(jnp.bfloat16)


def near_sums(window, pair_list, lower_slot, upper_slot, window_start, target_start, leaves):
    row_count, window_width = window.shape
    leaf_grid = window.reshape(row_count, window_width // LEAF, LEAF)
    places = leaf_grid[0:3].astype(jnp.float32)
    vectors = leaf_grid[3:]
    capacity = pair_list.shape[1]
    blocks = (upper_slot - lower_slot + block_pairs - 1) // block_pairs

    def accumulate(block_idx, running):
        slot_ids = lower_slot + block_idx * block_pairs + jnp.arange(block_pairs, dtype=jnp.int32)
        live_mask = (slot_ids < upper_slot).astype(jnp.float32)
        clipped = jnp.minimum(slot_ids, capacity - 1)
        targets = pair_list[0, clipped]
        sources = pair_list[1, clipped]
        kernel = matern(places[:, targets - window_start], places[:, sources - window_start])
        increment = jnp.einsum(
            "vps,pts->vpt",
            vectors[:, sources - window_start],
            kernel,
            preferred_element_type=jnp.float32,
        )
        return running.at[:, targets - target_start, :].add(increment * live_mask[None, :, None])

    blank_sum = jnp.zeros((row_count - 3, leaves, LEAF), jnp.float32)
    return lax.fori_loop(0, blocks, accumulate, blank_sum)


def on_device(
    coords,
    rhs,
    leaf_basis,
    low_transfer,
    low_pairs,
    low_blocks,
    upper_transfer,
    upper_pairs,
    upper_blocks,
    near_pairs,
    near_count,
):
    device = lax.axis_index(("grp", "sub"))
    devices = lax.axis_size(("grp", "sub"))
    vector_count, points = rhs.shape
    rank_size = leaf_basis.shape[0]
    leaves = points // LEAF
    tree_depth = leaves.bit_length() - 1
    upper_depth = devices.bit_length() - 1
    low_count = 2 * leaves - 2
    stacked = jnp.concatenate([coords, rhs], axis=0)
    basis_grid = leaf_basis.reshape(rank_size, leaves, LEAF)
    rhs_grid = rhs.reshape(vector_count, leaves, LEAF)
    current = jnp.einsum("rlp,vlp->lrv", basis_grid, rhs_grid, preferred_element_type=jnp.float32)
    tables = [current]
    start_at = 0
    breadth = leaves
    for height in range(tree_depth):
        lifted = jnp.einsum(
            "nrs,nrv->nsv",
            low_transfer[start_at : start_at + breadth].astype(jnp.float32),
            current,
            precision=highest,
        )
        current = lifted[0::2] + lifted[1::2]
        tables.append(current)
        start_at += breadth
        breadth //= 2
    low_table = jnp.concatenate(tables[:-1], axis=0)
    root_coef = current
    root_all = lax.all_gather(root_coef, ("grp", "sub"), axis=0, tiled=True)
    upper_levels = [root_all]
    current = root_all
    start_at = 0
    breadth = devices
    for height in range(upper_depth):
        lifted = jnp.einsum(
            "nrs,nrv->nsv",
            upper_transfer[start_at : start_at + breadth].astype(jnp.float32),
            current,
            precision=highest,
        )
        current = lifted[0::2] + lifted[1::2]
        upper_levels.append(current)
        start_at += breadth
        breadth //= 2
    upper_levels.append(jnp.zeros((1, rank_size, vector_count), jnp.float32))
    upper_table = jnp.concatenate(upper_levels, axis=0)
    coupled_up = jnp.einsum(
        "kab,kbv->kav",
        upper_blocks.astype(jnp.float32),
        upper_table[upper_pairs[1]],
        precision=highest,
    )
    selector_up = (
        jnp.arange(2 * devices, dtype=jnp.int32)[:, None] == upper_pairs[0][None, :]
    ).astype(jnp.float32)
    partial_up = jnp.dot(
        selector_up,
        coupled_up.reshape(coupled_up.shape[0], rank_size * vector_count),
        precision=highest,
    )
    partial_up = partial_up.reshape(2 * devices, rank_size, vector_count)
    summed = lax.psum(partial_up, ("grp", "sub"))
    root_down = summed[2 * devices - 2 : 2 * devices - 1]
    for height in reversed(range(upper_depth)):
        breadth = devices >> height
        position = 2 * devices - 2 * breadth + (device >> height)
        transfer_one = lax.dynamic_slice_in_dim(upper_transfer, position, 1, 0).astype(jnp.float32)
        local_one = lax.dynamic_slice_in_dim(summed, position, 1, 0)
        root_down = local_one + jnp.einsum(
            "nrs,nsv->nrv", transfer_one, root_down, precision=highest
        )
    coef_window = padded(low_table, ((("grp", "sub"), 0),), low_count)
    source_local = low_pairs[1] - (device - 1) * low_count
    target_local = low_pairs[0] - device * low_count
    coupled_low = jnp.einsum(
        "kab,kbv->kav", low_blocks.astype(jnp.float32), coef_window[source_local], precision=highest
    )
    selector_low = (
        jnp.arange(low_count, dtype=jnp.int32)[:, None] == target_local[None, :]
    ).astype(jnp.float32)
    low_far = jnp.dot(
        selector_low,
        coupled_low.reshape(coupled_low.shape[0], rank_size * vector_count),
        precision=highest,
    )
    low_far = low_far.reshape(low_count, rank_size, vector_count)
    current = root_down
    for height in reversed(range(tree_depth)):
        breadth = leaves >> height
        start_at = 2 * leaves - 2 * breadth
        spread = jnp.repeat(current, 2, axis=0)
        current = low_far[start_at : start_at + breadth] + jnp.einsum(
            "nrs,nsv->nrv",
            low_transfer[start_at : start_at + breadth].astype(jnp.float32),
            spread,
            precision=highest,
        )
    leaf_down = current.astype(jnp.bfloat16)
    far_field = jnp.einsum(
        "lrv,rlp->vlp", leaf_down, basis_grid, preferred_element_type=jnp.float32
    )
    window = padded(stacked, ((("grp", "sub"), 1),), points)
    near_total = near_sums(
        window, near_pairs, 0, near_count[0], (device - 1) * leaves, device * leaves, leaves
    )
    return (far_field + near_total).reshape(vector_count, points)


def solution(mesh):
    in_specs = (
        P(None, ("grp", "sub")),
        P(None, ("grp", "sub")),
        P(None, ("grp", "sub")),
        P(("grp", "sub"), None, None),
        P(None, ("grp", "sub")),
        P(("grp", "sub"), None, None),
        P(),
        P(None, ("grp", "sub")),
        P(("grp", "sub"), None, None),
        P(None, ("grp", "sub")),
        P(("grp", "sub")),
    )
    out_specs = P(None, ("grp", "sub"))
    return jax.shard_map(
        on_device, mesh=mesh, in_specs=in_specs, out_specs=out_specs, check_vma=False
    )
```

profile of v0, /device:TPU:1, one launch (start us, length us, event | category | flops | bytes accessed | tf_op | source)
XLA Modules:
  0.0 465.4 jit_solution(3273850028978277056)
XLA Ops:
  8.2 5.1 %collective-permute-start.3 = (bf16[35,2048]{1,0:T(8,128)(2,1)}, bf16[35,2048]{1,0:T(8,128)(2,1)}, u32[]{:S(2)}, u32[]{:S(2)}) collective-permute-start(bf16[35,2048]{1,0:T(8,128)(2,1)} %pad_maximum_fusion.4), channel_id=1, source_target_pairs={{1,0},{2,1},{3,2},{4,3},{5,4},{6,5},{7,6},{8,7},{9,8},{10,9},{11,1... | collective-permute-start | bytes 430088 | tf_op jit(solution)/shard_map/ppermute | solution.py:23
  23.1 2.9 collective-permute-start.1
  26.7 2.4 slice.188
  40.1 10.3 %constant_dynamic-slice_fusion.7 = (bf16[1,64,64]{0,2,1:T(8,128)(2,1)}, bf16[1,64,64]{0,2,1:T(8,128)(2,1)}, bf16[1,64,64]{0,2,1:T(8,128)(2,1)}, bf16[1,64,64]{0,...) fusion(bf16[510,64,64]{0,2,1:T(8,128)(2,1)} %param.19, ...), kind=kLoop, calls=%fused_computation.146 | loop fusion | bytes 131104 | tf_op jit(solution)/shard_map/dynamic_slice | solution.py:142
  50.4 6.7 %copy.139 = bf16[256,64,64]{2,1,0:T(8,128)(2,1)} copy(bf16[256,64,64]{0,2,1:T(8,128)(2,1)S(1)} %slice-done) | data formatting | bytes 4194304
  57.1 3.9 copy.140
  61.0 3.7 copy.141
  64.8 2.8 copy.142
  71.6 2.4 copy.145
  74.0 2.3 copy.146
  78.6 2.3 copy.153
  80.9 2.3 copy.152
  85.5 2.3 copy.150
  104.0 2.4 copy.100
  112.1 28.0 %all-gather.2.cloned.1.call-done = f32[256,64,32]{1,2,0:T(8,128)} async-done(((f32[1,64,32]{1,2,0:T(8,128)}), f32[256,64,32]{1,2,0:T(8,128)}) %all-gather.2.cloned.1.call-update) | async-done | bytes 2097168 | tf_op jit(solution)/shard_map/all_gather | solution.py:104
  140.1 4.9 %constant_dynamic-update-slice_fusion.9 = f32[512,64,32]{1,2,0:T(8,128)} fusion(f32[256,64,32]{1,2,0:T(8,128)} %all-gather.2.cloned.1.call-done), kind=kLoop, calls=%fused_computation.117 | loop fusion | bytes 6291456
  146.3 3.5 convolution_bitcast_fusion
  162.2 4.1 gather_fusion.6
  167.1 3.8 fusion.47
  171.1 48.8 %while.10 = (s32[]{:T(128)}, f32[32,8,256]{2,0,1:T(8,128)S(1)}, s32[]{:T(128)}, s32[2,80]{1,0:T(2,128)S(1)}, s32[]{:T(128)}, /*index=5*/s32[]{:T(128)}, f32[3,24...) while((s32[]{:T(128)}, f32[32,8,256]{2,0,1:T(8,128)S(1)}, ...), condition=%wide.region_3.4_spmd, body=%wide.region_1.3_spmd.sunk | while | flops 164105152 | bytes 7154713 | solution.py:60
  175.4 9.7 %fusion.96 = f32[32,32,256]{2,1,0:T(8,128)S(1)} fusion(f32[32,256]{1,0:T(8,128)S(1)} %bitcast.230, f32[32,256]{1,0:T(8,128)S(1)} %bitcast.231, f32[32,256]{1,0:T(8,128)S(1)} %bitcast.232, f32[32,256]{1,0:T(8,128)S(1)} %bitcast.233, f32[32,256]{1,0:T(8,128)S(1)} %bitcast.234, f32[32,256]{1,0:T(8,128)S(1)} %bitcast.235, ...), kind=kOutput, calls=%fused_computation.11.clone.1 | convolution fusion | flops 163840000 | bytes 1769600 | tf_op jit(solution)/shard_map/while/body/vps,pts->vpt/dot_general | solution.py:51
  191.6 9.7 %fusion.96 = f32[32,32,256]{2,1,0:T(8,128)S(1)} fusion(f32[32,256]{1,0:T(8,128)S(1)} %bitcast.230, f32[32,256]{1,0:T(8,128)S(1)} %bitcast.231, f32[32,256]{1,0:T(8,128)S(1)} %bitcast.232, f32[32,256]{1,0:T(8,128)S(1)} %bitcast.233, f32[32,256]{1,0:T(8,128)S(1)} %bitcast.234, f32[32,256]{1,0:T(8,128)S(1)} %bitcast.235, ...), kind=kOutput, calls=%fused_computation.11.clone.1 | convolution fusion | flops 163840000 | bytes 1769600 | tf_op jit(solution)/shard_map/while/body/vps,pts->vpt/dot_general | solution.py:51
  207.8 9.7 %fusion.96 = f32[32,32,256]{2,1,0:T(8,128)S(1)} fusion(f32[32,256]{1,0:T(8,128)S(1)} %bitcast.230, f32[32,256]{1,0:T(8,128)S(1)} %bitcast.231, f32[32,256]{1,0:T(8,128)S(1)} %bitcast.232, f32[32,256]{1,0:T(8,128)S(1)} %bitcast.233, f32[32,256]{1,0:T(8,128)S(1)} %bitcast.234, f32[32,256]{1,0:T(8,128)S(1)} %bitcast.235, ...), kind=kOutput, calls=%fused_computation.11.clone.1 | convolution fusion | flops 163840000 | bytes 1769600 | tf_op jit(solution)/shard_map/while/body/vps,pts->vpt/dot_general | solution.py:51
  219.9 215.3 %all-reduce.4.cloned.1.call-done = f32[512,64,32]{0,1,2:T(8,128)} async-done(((f32[512,64,32]{0,1,2:T(8,128)}), f32[512,64,32]{0,1,2:T(8,128)}) %all-reduce.4.cloned.1.call-update) | async-done | bytes 4194320 | tf_op jit(solution)/shard_map/psum | solution.py:137
  (232 shorter events, 109.2 us)
Async XLA Ops:
  6.5 95.7 %copy-start = (bf16[32,64,64]{2,1,0:T(8,128)(2,1)S(1)}, bf16[32,64,64]{2,1,0:T(8,128)(2,1)}, u32[]{:S(2)}) copy-start(bf16[32,64,64]{2,1,0:T(8,128)(2,1)} %param.18) | copy-start | bytes 786436
  6.5 133.6 %all-gather.2.cloned.1.call-start = ((), (), s32[]{:S(2)}) async-start(), calls=%async_computation | async-start | bytes 4210688 | tf_op jit(solution)/shard_map/all_gather | solution.py:104
  8.2 101.9 %collective-permute-start.3 = (bf16[35,2048]{1,0:T(8,128)(2,1)}, bf16[35,2048]{1,0:T(8,128)(2,1)}, u32[]{:S(2)}, u32[]{:S(2)}) collective-permute-start(bf16[35,2048]{1,0:T(8,128)(2,1)} %pad_maximum_fusion.4), channel_id=1, source_target_pairs={{1,0},{2,1},{3,2},{4,3},{5,4},{6,5},{7,6},{8,7},{9,8},{10,9},{11,1... | collective-permute-start | bytes 430088 | tf_op jit(solution)/shard_map/ppermute | solution.py:23
  13.4 96.8 %collective-permute-start.2 = (bf16[35,2048]{1,0:T(8,128)(2,1)}, bf16[35,2048]{1,0:T(8,128)(2,1)}, u32[]{:S(2)}, u32[]{:S(2)}) collective-permute-start(bf16[35,2048]{1,0:T(8,128)(2,1)} %pad_maximum_fusion.4), channel_id=1, source_target_pairs={{0,1},{1,2},{2,3},{3,4},{4,5},{5,6},{6,7},{7,8},{8,9},{9,10},{10,1... | collective-permute-start | bytes 430088 | tf_op jit(solution)/shard_map/ppermute | solution.py:22
  20.2 414.9 %all-reduce.4.cloned.1.call-start = ((), (), s32[]{:S(2)}) async-start(), calls=%async_computation.1 | async-start | bytes 8388608 | tf_op jit(solution)/shard_map/psum | solution.py:137
  21.0 74.2 %collective-permute-start = (f32[14,64,32]{1,2,0:T(8,128)}, f32[14,64,32]{1,2,0:T(8,128)}, u32[]{:S(2)}, u32[]{:S(2)}) collective-permute-start(f32[14,64,32]{1,2,0:T(8,128)} %pad_maximum_fusion.3), channel_id=1, source_target_pairs={{0,1},{1,2},{2,3},{3,4},{4,5},{5,6},{6,7},{7,8},{8,9},{9,10},{10,1... | collective-permute-start | bytes 344072 | tf_op jit(solution)/shard_map/ppermute | solution.py:22
  23.1 75.6 %collective-permute-start.1 = (f32[14,64,32]{1,2,0:T(8,128)}, f32[14,64,32]{1,2,0:T(8,128)}, u32[]{:S(2)}, u32[]{:S(2)}) collective-permute-start(f32[14,64,32]{1,2,0:T(8,128)} %pad_maximum_fusion.3), channel_id=1, source_target_pairs={{1,0},{2,1},{3,2},{4,3},{5,4},{6,5},{7,6},{8,7},{9,8},{10,9},{11,1... | collective-permute-start | bytes 344072 | tf_op jit(solution)/shard_map/ppermute | solution.py:23
  80.9 29.3 %copy-start.8 = (bf16[32,2048]{1,0:T(8,128)(2,1)S(1)}, bf16[32,2048]{1,0:T(8,128)(2,1)}, u32[]{:S(2)}) copy-start(bf16[32,2048]{1,0:T(8,128)(2,1)} %param.14) | copy-start | bytes 393220
  80.9 29.3 %copy-start.13 = (bf16[3,2048]{1,0:T(4,128)(2,1)S(1)}, bf16[3,2048]{1,0:T(4,128)(2,1)}, u32[]{:S(2)}) copy-start(bf16[3,2048]{1,0:T(4,128)(2,1)} %param.13) | copy-start | bytes 36868
  151.7 14.5 %copy-start.14 = (bf16[8,64,64]{2,1,0:T(8,128)(2,1)S(1)}, bf16[8,64,64]{2,1,0:T(8,128)(2,1)}, u32[]{:S(2)}) copy-start(bf16[8,64,64]{2,1,0:T(8,128)(2,1)} %param.21) | copy-start | bytes 196612
  153.8 13.4 %copy-start.25 = (s32[8]{0:T(128)S(1)}, s32[8]{0:T(128)}, u32[]{:S(2)}) copy-start(s32[8]{0:T(128)} %slice_bitcast_fusion) | copy-start | bytes 100
  155.9 15.1 %copy-start.2 = (s32[2,80]{1,0:T(2,128)S(1)}, s32[2,80]{1,0:T(2,128)}, u32[]{:S(2)}) copy-start(s32[2,80]{1,0:T(2,128)} %param.22) | copy-start | bytes 1924
  171.0 266.0 %copy-start.17 = (bf16[1,64,64]{2,1,0:T(8,128)(2,1)S(1)}, bf16[1,64,64]{2,1,0:T(8,128)(2,1)}, u32[]{:S(2)}) copy-start(bf16[1,64,64]{2,1,0:T(8,128)(2,1)} %copy.154) | copy-start | bytes 24580
  171.0 268.4 %copy-start.18 = (bf16[1,64,64]{2,1,0:T(8,128)(2,1)S(1)}, bf16[1,64,64]{2,1,0:T(8,128)(2,1)}, u32[]{:S(2)}) copy-start(bf16[1,64,64]{2,1,0:T(8,128)(2,1)} %copy.153) | copy-start | bytes 24580
  171.0 270.9 %copy-start.19 = (bf16[1,64,64]{2,1,0:T(8,128)(2,1)S(1)}, bf16[1,64,64]{2,1,0:T(8,128)(2,1)}, u32[]{:S(2)}) copy-start(bf16[1,64,64]{2,1,0:T(8,128)(2,1)} %copy.152) | copy-start | bytes 24580
  219.8 224.6 %copy-start.20 = (bf16[1,64,64]{2,1,0:T(8,128)(2,1)S(1)}, bf16[1,64,64]{2,1,0:T(8,128)(2,1)}, u32[]{:S(2)}) copy-start(bf16[1,64,64]{2,1,0:T(8,128)(2,1)} %copy.151) | copy-start | bytes 24580
  219.8 227.0 %copy-start.21 = (bf16[1,64,64]{2,1,0:T(8,128)(2,1)S(1)}, bf16[1,64,64]{2,1,0:T(8,128)(2,1)}, u32[]{:S(2)}) copy-start(bf16[1,64,64]{2,1,0:T(8,128)(2,1)} %copy.150) | copy-start | bytes 24580
  219.8 229.5 %copy-start.22 = (bf16[1,64,64]{2,1,0:T(8,128)(2,1)S(1)}, bf16[1,64,64]{2,1,0:T(8,128)(2,1)}, u32[]{:S(2)}) copy-start(bf16[1,64,64]{2,1,0:T(8,128)(2,1)} %copy.149) | copy-start | bytes 24580
  439.5 12.3 %copy-start.23 = (bf16[1,64,64]{2,1,0:T(8,128)(2,1)S(1)}, bf16[1,64,64]{2,1,0:T(8,128)(2,1)}, u32[]{:S(2)}) copy-start(bf16[1,64,64]{2,1,0:T(8,128)(2,1)} %copy.148) | copy-start | bytes 24580
  441.9 12.3 %copy-start.24 = (bf16[1,64,64]{2,1,0:T(8,128)(2,1)S(1)}, bf16[1,64,64]{2,1,0:T(8,128)(2,1)}, u32[]{:S(2)}) copy-start(bf16[1,64,64]{2,1,0:T(8,128)(2,1)} %copy.147) | copy-start | bytes 24580
  444.4 12.3 %copy-start.9 = (bf16[14,64,64]{2,1,0:T(8,128)(2,1)S(1)}, bf16[14,64,64]{2,1,0:T(8,128)(2,1)}, u32[]{:S(2)}) copy-start(bf16[14,64,64]{2,1,0:T(8,128)(2,1)} %param.16) | copy-start | bytes 344068
  444.4 12.3 %copy-start.15 = (f32[2,64,32]{1,2,0:T(8,128)S(1)}, f32[2,64,32]{1,2,0:T(8,128)}, u32[]{:S(2)}) copy-start(f32[2,64,32]{1,2,0:T(8,128)} %copy.127) | copy-start | bytes 49156
  444.5 12.9 %copy-start.12 = (bf16[64,2048]{1,0:T(8,128)(2,1)S(1)}, bf16[64,2048]{1,0:T(8,128)(2,1)}, u32[]{:S(2)}) copy-start(bf16[64,2048]{1,0:T(8,128)(2,1)} %param.15) | copy-start | bytes 786436
  444.6 13.8 %copy-start.1 = (bf16[32,64,64]{2,1,0:T(8,128)(2,1)S(1)}, bf16[32,64,64]{2,1,0:T(8,128)(2,1)}, u32[]{:S(2)}) copy-start(bf16[32,64,64]{2,1,0:T(8,128)(2,1)} %param.18) | copy-start | bytes 786436
  (11 other events, 85.3 us)
Sparse Core Ops, SparseCore 0:
  20.3 119.7 all-gather.1
  171.1 263.9 all-reduce.3
where the time goes:
time: 474 us; the launch traced here: 465 us
  waiting for transfers between devices  243 us (51%)
  local copies, waits for them, and re-layouts  106 us (22%)
  matrix products  49.7 us (10%)
  other arithmetic  38.6 us (8%)
  between operations  15 us (3%)
  starting transfers between devices  12.1 us (3%)
    psum x1, waiting for transfers between devices, on_device(): summed = lax.psum(partial_up, ('grp', 'sub'))  215 us
    unnamed x75, local copies, waits for them, and re-layouts  52.8 us
    dot_general x3, matrix products, accumulate(): jnp.einsum('vps,pts->vpt', vectors[:, sources - window_start], kernel, pr...  29 us
    all_gather x1, waiting for transfers between devices, on_device(): root_all = lax.all_gather(root_coef, ('grp', 'sub'), axis=0, tiled=True)  28 us
    add x8, other arithmetic, on_device(): local_one + jnp.einsum('nrs,nsv->nrv', transfer_one, root_down, precision...  15 us
    slice x9, local copies, waits for them, and re-layouts, on_device(): upper_transfer[start_at:start_at + breadth].astype(jnp.float32)  11.6 us
    dynamic_slice x1, local copies, waits for them, and re-layouts, on_device(): lax.dynamic_slice_in_dim(upper_transfer, position, 1, 0).astype(jnp.float32)  10.3 us
  transfers between devices with their start and end apart: 6, of which 2 were waited for; matrix products, arithmetic and copies ran while one was open for 30% of the time, Pallas kernels for 0%

commit v1 on v0

v1 whole, which is shorter than its diff:
```python
import jax
import jax.numpy as jnp
from jax import lax
from jax.experimental import pallas as pl
from jax.experimental.pallas import tpu as pltpu
from jax.sharding import PartitionSpec as P

LEAF = 256
MEMB = 16
ROWS = 40
C2 = 6.244106943016823
AMP = 0.0625
LN2 = 0.6931471805599453
MESH = pl.DeviceIdType.MESH
F32 = jnp.float32
BF16 = jnp.bfloat16


def dot(a, b, nt=False):
    dims = (((1,), (1,)), ((), ())) if nt else (((1,), (0,)), ((), ()))
    return lax.dot_general(a, b, dims, preferred_element_type=F32)


def split2(c):
    hi = c.astype(BF16)
    lo = (c - hi.astype(F32)).astype(BF16)
    return jnp.concatenate([hi, lo], axis=0)


def dot2(c, w, nt=False):
    n = c.shape[0]
    r = dot(split2(c), w, nt)
    return r[:n] + r[n:]


def pack(c):
    h = c.shape[0] // 2
    return jnp.concatenate([c[:h], c[h:]], axis=1)


def unpack(p):
    h = p.shape[1] // 2
    return jnp.concatenate([p[:, :h], p[:, h:]], axis=0)


def split3(x):
    a = x.astype(BF16).astype(F32)
    y = x - a
    b = y.astype(BF16).astype(F32)
    return a, b, (y - b).astype(BF16).astype(F32)


def features(xyz):
    x, y, z = xyz[0:1], xyz[1:2], xyz[2:3]
    norm = C2 * (x * x + y * y + z * z)
    n = split3(norm)
    m = [split3(-2.0 * C2 * v) for v in (x, y, z)]
    one = jnp.ones_like(x)
    zero = jnp.zeros_like(x)
    tgt = [x, y, z] * 3 + list(n) + [one] * 3 + [zero]
    src = [m[c][part] for part in range(3) for c in range(3)] + [one] * 3 + list(n) + [zero]
    row = lax.broadcasted_iota(jnp.int32, (16, xyz.shape[1]), 0)

    def build(rows):
        out = jnp.zeros((16, xyz.shape[1]), F32)
        for i, v in enumerate(rows[:15]):
            out = jnp.where(row == i, v, out)
        return out.astype(BF16)

    return build(tgt), build(src)


def up_levels(leaves, values, weights):
    out = list(values)
    start, breadth = 0, leaves
    while breadth > 1:
        for i in range(breadth // 2):
            left, right = start + 2 * i, start + 2 * i + 1
            out.append(dot2(out[left], weights(left)) + dot2(out[right], weights(right)))
        start += breadth
        breadth //= 2
    return out


def far_kernel(
    groups,
    coords_ref,
    rhs_ref,
    basis_ref,
    lt_ref,
    pairs_ref,
    ub_ref,
    ut_ref,
    rootd_ref,
    lowwin_ref,
    ft_ref,
    fswin_ref,
    rhswin_ref,
    eg_ref,
    req_ref,
    tab_ref,
    send2_ref,
    recv2_ref,
    s_ref,
    pr_ref,
    send3_ref,
    recv3_ref,
    tabd_ref,
    send4_ref,
    recv4_ref,
    oh3_ref,
    eg_sem,
    halo_s,
    halo_r,
    req_s,
    req_r,
    p1_s,
    p1_r,
    p2_s,
    p2_r,
    p3_s,
    p3_r,
    p4_s,
    p4_r,
):
    ndev = groups * MEMB
    subs = lax.axis_size("sub")
    per_row = subs // MEMB
    yy = lax.axis_index("grp")
    sub = lax.axis_index("sub")
    dev = yy * subs + sub
    g = dev // MEMB
    m = dev % MEMB

    def at_dev(d):
        return (d // subs, d % subs)

    def other_group(i):
        return (g + i) % groups

    def other_member(i):
        return (m + i) % MEMB

    barrier = pltpu.get_barrier_semaphore()

    def greet_group(i, c):
        pl.semaphore_signal(barrier, inc=1, device_id=at_dev(other_group(i) * MEMB + m), device_id_type=MESH)
        return c

    def greet_member(i, c):
        pl.semaphore_signal(barrier, inc=1, device_id=at_dev(g * MEMB + other_member(i)), device_id_type=MESH)
        return c

    after, before = (dev + 1) % ndev, (dev + ndev - 1) % ndev
    lax.fori_loop(1, groups, greet_group, 0)
    lax.fori_loop(1, MEMB, greet_member, 0)
    for d in (after, before):
        pl.semaphore_signal(barrier, inc=1, device_id=at_dev(d), device_id_type=MESH)

    depth = ndev.bit_length() - 1
    copies = []
    row = 0
    for level in range(min(7, depth - 1)):
        base = 2 * ndev - 2 * (ndev >> level)
        count = max(1, MEMB >> level)
        at = base + (g * count if level <= 4 else g // (1 << (level - 4)))
        copies.append(
            pltpu.make_async_copy(ut_ref.at[pl.ds(at, count)], eg_ref.at[pl.ds(row, count)], eg_sem.at[level])
        )
        copies[-1].start()
        row += count

    srow = lax.broadcasted_iota(jnp.int32, (8, 128), 0)
    slane = lax.broadcasted_iota(jnp.int32, (8, 128), 1)
    tile = jnp.zeros((8, 128), jnp.int32)
    for i in range(8):
        tile = jnp.where(srow == i, jnp.where(slane < 64, pairs_ref[1, i], pairs_ref[0, i]), tile)
    req_ref[g] = tile

    leaves = rhs_ref.shape[1] // LEAF
    first = [
        dot(rhs_ref[:, l * LEAF : (l + 1) * LEAF], basis_ref[:, l * LEAF : (l + 1) * LEAF], nt=True)
        for l in range(leaves)
    ]
    low = up_levels(leaves, first, lambda i: lt_ref[i])
    for i in range(2 * leaves - 2):
        lowwin_ref[1, i] = low[i]
    tab_ref[MEMB * 16 :, :] = jnp.zeros(((ROWS - MEMB) * 16, 128), F32)
    mine = pl.ds(pl.multiple_of(m * 16, 16), 16)
    tab_ref[mine, :] = pack(low[-1])
    ft, fs = features(coords_ref[...].astype(F32))
    ft_ref[...] = ft
    fswin_ref[1] = fs
    rhswin_ref[1] = rhs_ref[...]

    pl.semaphore_wait(barrier, groups - 1 + MEMB - 1 + 2)

    def copy1(i):
        return pltpu.make_async_remote_copy(
            tab_ref.at[mine], tab_ref.at[mine], p1_s.at[i], p1_r.at[i],
            device_id=at_dev(g * MEMB + other_member(i)), device_id_type=MESH)

    def copy_req(i):
        return pltpu.make_async_remote_copy(
            req_ref.at[g], req_ref.at[g], req_s.at[i], req_r.at[i],
            device_id=at_dev(other_group(i) * MEMB + m), device_id_type=MESH)

    def start(copy, lo, hi):
        def body(i, c):
            copy(i).start()
            return c
        lax.fori_loop(lo, hi, body, 0)

    def await_recv(copy, lo, hi):
        def body(i, c):
            copy(i).wait_recv()
            return c
        lax.fori_loop(lo, hi, body, 0)

    def await_send(copy, lo, hi):
        def body(i, c):
            copy(i).wait_send()
            return c
        lax.fori_loop(lo, hi, body, 0)

    start(copy1, 1, MEMB)
    start(copy_req, 1, groups)
    halo = []
    for side, to in ((0, after), (2, before)):
        for j, ref in enumerate((lowwin_ref, fswin_ref, rhswin_ref)):
            k = (side // 2) * 3 + j
            halo.append(
                pltpu.make_async_remote_copy(
                    ref.at[1], ref.at[side], halo_s.at[k], halo_r.at[k],
                    device_id=at_dev(to), device_id_type=MESH))
    for c in halo:
        c.start()

    lane = lax.broadcasted_iota(jnp.int32, (1, 2 * ROWS), 1)
    half = lane // ROWS
    trow = lane % ROWS
    cid = jnp.full((1, 2 * ROWS), -1, jnp.int32)
    row = 0
    for level in range(depth):
        base = 2 * ndev - 2 * (ndev >> level)
        count = max(1, MEMB >> level)
        at = base + (g * count if level <= 4 else g // (1 << (level - 4)))
        cid = jnp.where((trow >= row) & (trow < row + count), at + trow - row, cid)
        row += count

    await_recv(copy_req, 1, groups)

    def onehot(column):
        pieces = []
        for other in range(groups):
            eq = (column[other] == cid).astype(F32)
            for part in range(2):
                pieces.append(jnp.where(half == part, eq, 0.0))
        return jnp.concatenate(pieces, axis=0)

    req = req_ref[...]
    oh2 = onehot([req[o][:, 0:1] for o in range(groups)]).astype(BF16)
    oh3_ref[...] = jnp.transpose(onehot([req[o][:, 64:65] for o in range(groups)])).astype(BF16)

    for c in copies:
        c.wait()
    await_recv(copy1, 1, MEMB)

    roots = [unpack(tab_ref[i * 16 : (i + 1) * 16, :]) for i in range(MEMB)]
    table = up_levels(MEMB, roots, lambda i: eg_ref[i])
    for level in range(5, depth):
        table.append(dot2(table[-1], eg_ref[len(table) - 1]))
    for i in range(MEMB, len(table)):
        tab_ref[i * 16 : (i + 1) * 16, :] = pack(table[i])

    for vq in range(8):
        t = jnp.concatenate([tab_ref[pl.ds(vs * 8 + vq, ROWS, stride=16), :] for vs in range(2)], axis=0)
        out = dot(oh2, t.astype(BF16)).astype(BF16)
        send2_ref[:, vq * 16 : (vq + 1) * 16, :] = out.reshape(groups, 16, 128)
    recv2_ref[g] = send2_ref[g]

    def copy2(i):
        return pltpu.make_async_remote_copy(
            send2_ref.at[other_group(i)], recv2_ref.at[g], p2_s.at[i], p2_r.at[i],
            device_id=at_dev(other_group(i) * MEMB + m), device_id_type=MESH)

    start(copy2, 1, groups)
    await_recv(copy2, 1, groups)
    total = recv2_ref[0].astype(F32)
    for o in range(1, groups):
        total = total + recv2_ref[o].astype(F32)
    s_ref[...] = total

    for i in range(8):
        x = jnp.concatenate([s_ref[pl.ds(vs * 8 + i, 8, stride=16), :] for vs in range(2)], axis=0)
        pr_ref[i * 16 : (i + 1) * 16, :] = pack(dot2(unpack(x), ub_ref[i], nt=True))
    send3_ref[...] = jnp.concatenate(
        [pr_ref[pl.ds(vs * 8 + vq, 8, stride=16), :] for vq in range(8) for vs in range(2)], axis=0
    ).astype(BF16)
    recv3_ref[g] = send3_ref[...]

    def copy3(i):
        return pltpu.make_async_remote_copy(
            send3_ref, recv3_ref.at[g], p3_s.at[i], p3_r.at[i],
            device_id=at_dev(other_group(i) * MEMB + m), device_id_type=MESH)

    start(copy3, 1, groups)
    await_recv(copy3, 1, groups)

    oh3 = oh3_ref[...]
    for vq in range(8):
        r = recv3_ref[:, vq * 16 : (vq + 1) * 16, :].reshape(groups * 16, 128)
        tabd_ref[vq * 2 * ROWS : (vq + 1) * 2 * ROWS, :] = dot(oh3, r)

    def summed(c):
        return unpack(
            jnp.concatenate([tabd_ref[pl.ds(vs * ROWS + c, 8, stride=2 * ROWS), :] for vs in range(2)], axis=0)
        )

    at = len(table) - 1
    down = summed(at)
    while at > 2 * MEMB - 2:
        at -= 1
        down = summed(at) + dot2(down, eg_ref[at], nt=True)
    current = [down]
    breadth = 2
    while breadth <= MEMB:
        at = 2 * MEMB - 2 * breadth
        current = [summed(at + i) + dot2(current[i // 2], eg_ref[at + i], nt=True) for i in range(breadth)]
        breadth *= 2
    for i in range(MEMB):
        send4_ref[i] = pack(current[i])
    recv4_ref[m] = send4_ref[m]

    def copy4(i):
        return pltpu.make_async_remote_copy(
            send4_ref.at[other_member(i)], recv4_ref.at[m], p4_s.at[i], p4_r.at[i],
            device_id=at_dev(g * MEMB + other_member(i)), device_id_type=MESH)

    start(copy4, 1, MEMB)
    await_recv(copy4, 1, MEMB)
    total = recv4_ref[0]
    for i in range(1, MEMB):
        total = total + recv4_ref[i]
    rootd_ref[...] = total

    for c in halo:
        c.wait()
    await_send(copy_req, 1, groups)
    await_send(copy1, 1, MEMB)
    await_send(copy2, 1, groups)
    await_send(copy3, 1, groups)
    await_send(copy4, 1, MEMB)


def near_kernel(
    np_ref,
    nc_ref,
    lp_ref,
    ft_ref,
    fswin_ref,
    rhswin_ref,
    basis_ref,
    lt_ref,
    lb_ref,
    lowwin_ref,
    rootd_ref,
    out_ref,
    fst_ref,
    rw_ref,
    ftl_ref,
    acc_ref,
    lowacc_ref,
):
    dev = lax.axis_index("grp") * lax.axis_size("sub") + lax.axis_index("sub")
    leaves = out_ref.shape[1] // LEAF
    low_count = 2 * leaves - 2
    for i in range(low_count):
        lowacc_ref[i] = jnp.zeros(lowacc_ref.shape[1:], F32)
    for k in range(lp_ref.shape[1]):
        s = lp_ref[1, k] - (dev - 1) * low_count
        t = lp_ref[0, k] - dev * low_count
        prod = dot2(lowwin_ref[s // low_count, s % low_count], lb_ref[k], nt=True)
        lowacc_ref[t] = lowacc_ref[t] + prod
    current = [unpack(rootd_ref[...])]
    breadth = 2
    while breadth <= leaves:
        at = 2 * leaves - 2 * breadth
        current = [lowacc_ref[at + i] + dot2(current[i // 2], lt_ref[at + i], nt=True) for i in range(breadth)]
        breadth *= 2
    for l in range(leaves):
        acc_ref[l] = dot2(current[l], basis_ref[:, l * LEAF : (l + 1) * LEAF])
    for w in range(3):
        for l in range(leaves):
            cols = slice(l * LEAF, (l + 1) * LEAF)
            fst_ref[w * leaves + l] = jnp.transpose(fswin_ref[w, :, cols].astype(F32)).astype(BF16)
            rw_ref[w * leaves + l] = rhswin_ref[w, :, cols]
    for l in range(leaves):
        ftl_ref[l] = ft_ref[:, l * LEAF : (l + 1) * LEAF]

    def body(k, c):
        t = np_ref[0, k] - dev * leaves
        s = np_ref[1, k] - (dev - 1) * leaves
        sq = jnp.maximum(dot(fst_ref[s], ftl_ref[t]), 1e-30)
        p = sq * lax.rsqrt(sq)
        tile = ((AMP + (AMP * LN2) * p) * jnp.exp2(-p)).astype(BF16)
        acc_ref[t] = acc_ref[t] + dot(rw_ref[s], tile)
        return c

    lax.fori_loop(0, nc_ref[0], body, 0)
    for l in range(leaves):
        out_ref[:, l * LEAF : (l + 1) * LEAF] = acc_ref[l]


def on_device(coords, rhs, basis, lt, lp, lb, ut, up, ub, npairs, ncount):
    ndev = lax.axis_size(("grp", "sub"))
    groups = ndev // MEMB
    points = rhs.shape[1]
    leaves = points // LEAF
    low_count = 2 * leaves - 2
    vm = pl.BlockSpec(memory_space=pltpu.VMEM)
    sm = pl.BlockSpec(memory_space=pltpu.SMEM)
    dma = pltpu.SemaphoreType.DMA
    rootd, lowwin, ft, fswin, rhswin = pl.pallas_call(
        lambda *refs: far_kernel(groups, *refs),
        out_shape=[
            jax.ShapeDtypeStruct((16, 128), F32),
            jax.ShapeDtypeStruct((3, low_count, 32, 64), F32),
            jax.ShapeDtypeStruct((16, points), BF16),
            jax.ShapeDtypeStruct((3, 16, points), BF16),
            jax.ShapeDtypeStruct((3, 32, points), BF16),
        ],
        in_specs=[vm, vm, vm, vm, sm, vm, pl.BlockSpec(memory_space=pl.ANY)],
        out_specs=[vm] * 5,
        scratch_shapes=[
            pltpu.VMEM((ROWS, 64, 64), BF16),
            pltpu.VMEM((groups, 8, 128), jnp.int32),
            pltpu.VMEM((ROWS * 16, 128), F32),
            pltpu.VMEM((groups, 128, 128), BF16),
            pltpu.VMEM((groups, 128, 128), BF16),
            pltpu.VMEM((128, 128), F32),
            pltpu.VMEM((128, 128), F32),
            pltpu.VMEM((128, 128), BF16),
            pltpu.VMEM((groups, 128, 128), BF16),
            pltpu.VMEM((8 * 2 * ROWS, 128), F32),
            pltpu.VMEM((MEMB, 16, 128), F32),
            pltpu.VMEM((MEMB, 16, 128), F32),
            pltpu.VMEM((2 * ROWS, groups * 16), BF16),
            dma((8,)),
            dma((6,)),
            dma((6,)),
            dma((groups,)),
            dma((groups,)),
            dma((MEMB,)),
            dma((MEMB,)),
            dma((groups,)),
            dma((groups,)),
            dma((groups,)),
            dma((groups,)),
            dma((MEMB,)),
            dma((MEMB,)),
        ],
        compiler_params=pltpu.CompilerParams(
            collective_id=0, has_side_effects=True, vmem_limit_bytes=40 * 2**20
        ),
        name="far_exchange",
    )(coords, rhs, basis, lt, up, ub, ut)
    return pl.pallas_call(
        near_kernel,
        out_shape=jax.ShapeDtypeStruct((32, points), F32),
        in_specs=[sm, sm, sm] + [vm] * 8,
        out_specs=vm,
        scratch_shapes=[
            pltpu.VMEM((3 * leaves, LEAF, 16), BF16),
            pltpu.VMEM((3 * leaves, 32, LEAF), BF16),
            pltpu.VMEM((leaves, 16, LEAF), BF16),
            pltpu.VMEM((leaves, 32, LEAF), F32),
            pltpu.VMEM((low_count, 32, 64), F32),
        ],
        compiler_params=pltpu.CompilerParams(vmem_limit_bytes=40 * 2**20),
        name="near_field",
    )(npairs, ncount, lp, ft, fswin, rhswin, basis, lt, lb, lowwin, rootd)


def solution(mesh):
    both = ("grp", "sub")
    in_specs = (
        P(None, both), P(None, both), P(None, both), P(both), P(None, both), P(both),
        P(), P(None, both), P(both), P(None, both), P(both),
    )
    return jax.shard_map(on_device, mesh=mesh, in_specs=in_specs, out_specs=P(None, both), check_vma=False)
```

time: 474 us -> 85.4 us (0.18)
  the two profiles are of different devices: /device:TPU:1 before, /device:TPU:3 now
where the time goes in v1:
time: 85.4 us; the launch traced here: 85.1 us
  Pallas kernels  70.8 us (83%)
  local copies, waits for them, and re-layouts  13.5 us (16%)
    pallas_call x1, Pallas kernels, on_device(): pl.pallas_call(lambda *refs: far_kernel(groups, *refs), out_shape=[jax.Sh...  44.5 us
    pallas_call x1, Pallas kernels, on_device(): pl.pallas_call(near_kernel, out_shape=jax.ShapeDtypeStruct((32, points),...  26.3 us
    unnamed x21, local copies, waits for them, and re-layouts  13.5 us

profile of v1, /device:TPU:3, one launch (start us, length us, event | category | flops | bytes accessed | tf_op | source)
XLA Modules:
  0.0 85.1 jit_solution(4991504477134046901)
XLA Ops:
  0.0 0.0 copy-start.6
  0.0 0.0 copy-start.4
  0.0 0.0 copy-start.1
  0.0 0.0 copy-start.2
  0.0 0.0 copy-start.9
  0.0 0.0 copy-start.5
  0.0 0.0 copy-start.8
  0.0 0.0 copy-start.3
  0.1 0.0 copy-start.7
  0.1 10.1 %copy.12.refs_6_ = bf16[510,64,64]{2,1,0:T(8,128)(2,1)} copy(bf16[510,64,64]{0,2,1:T(8,128)(2,1)} %param.17) | data formatting | bytes 8355840 | tf_op args[6]
  10.2 0.0 copy-done.6
  10.2 0.0 copy-done.4
  10.2 0.0 copy-done.1
  10.2 0.0 copy-done.2
  10.2 0.0 copy-done.9
  10.2 0.0 copy-done.5
  10.2 0.0 copy-start
  10.2 3.4 %copy-done = bf16[510,64,64]{2,1,0:T(8,128)(2,1)S(1)} copy-done((bf16[510,64,64]{2,1,0:T(8,128)(2,1)S(1)}, bf16[510,64,64]{2,1,0:T(8,128)(2,1)}, u32[]{:S(2)}) %copy-start) | copy-done | bytes 4177944
  13.6 44.5 %far_exchange.1 = (f32[16,128]{1,0:T(8,128)S(1)}, f32[3,14,32,64]{3,2,1,0:T(8,128)S(1)}, bf16[16,2048]{1,0:T(8,128)(2,1)S(1)}, bf16[3,16,2048]{2,1,0:T(8,128)(2,1)S(1)}, bf16[3,32,2048]{2,1,0:T(8,128)(2,1)S(1)}) custom-call(bf16[3,2048]{1,0:T(4,128)(2,1)S(1)} %copy-done.6, bf16[32,2048]{1,0:T(8,128)(2,1)S(1)} %copy-done.4, bf16[64,2048]{1,0:T(8,128)(2,1)S(1)} %copy-done.1, ...), custom_call_target="tpu_custom_call" | custom-call | tf_op jit(solution)/shard_map/far_exchange/pallas_call | solution.py:424
  58.8 0.0 copy-done.8
  58.8 0.0 copy-done.3
  58.8 0.0 copy-done.7
  58.8 26.3 %near_field.1 = f32[32,2048]{1,0:T(8,128)} custom-call(s32[2,80]{1,0:T(2,128)S(1)} %copy-done.7, s32[1]{0:T(128)S(6)} %copy.13.nc_ref, s32[2,32]{1,0:T(2,128)S(1)} %copy-done.8, bf16[16,2048]{1,0:T(8,128)(2,1)S(1)} %get-tuple-element.10.ft_ref, bf16[3,16,2048]{2,1,0:T(8,128)(2,1)S(1)} %get-tuple-element.11.fswin_ref, ...), custom_call_target="tpu_custom_call" | custom-call | tf_op jit(solution)/shard_map/near_field/pallas_call | solution.py:468
Async XLA Ops:
  0.0 10.2 %copy-start.6 = (bf16[3,2048]{1,0:T(4,128)(2,1)S(1)}, bf16[3,2048]{1,0:T(4,128)(2,1)}, u32[]{:S(2)}) copy-start(bf16[3,2048]{1,0:T(4,128)(2,1)} %refs_0_.1) | copy-start | bytes 36868
  0.0 10.2 %copy-start.4 = (bf16[32,2048]{1,0:T(8,128)(2,1)S(1)}, bf16[32,2048]{1,0:T(8,128)(2,1)}, u32[]{:S(2)}) copy-start(bf16[32,2048]{1,0:T(8,128)(2,1)} %refs_1_.1) | copy-start | bytes 393220
  0.0 10.2 %copy-start.1 = (bf16[64,2048]{1,0:T(8,128)(2,1)S(1)}, bf16[64,2048]{1,0:T(8,128)(2,1)}, u32[]{:S(2)}) copy-start(bf16[64,2048]{1,0:T(8,128)(2,1)} %basis_ref.1) | copy-start | bytes 786436
  0.0 10.2 %copy-start.2 = (bf16[14,64,64]{2,1,0:T(8,128)(2,1)S(1)}, bf16[14,64,64]{2,1,0:T(8,128)(2,1)}, u32[]{:S(2)}) copy-start(bf16[14,64,64]{2,1,0:T(8,128)(2,1)} %lt_ref.1) | copy-start | bytes 344068
  0.0 10.2 %copy-start.9 = (s32[2,8]{1,0:T(2,128)S(1)}, s32[2,8]{1,0:T(2,128)}, u32[]{:S(2)}) copy-start(s32[2,8]{1,0:T(2,128)} %refs_4_.1) | copy-start | bytes 196
  0.0 10.2 %copy-start.5 = (bf16[8,64,64]{2,1,0:T(8,128)(2,1)S(1)}, bf16[8,64,64]{2,1,0:T(8,128)(2,1)}, u32[]{:S(2)}) copy-start(bf16[8,64,64]{2,1,0:T(8,128)(2,1)} %refs_5_.1) | copy-start | bytes 196612
  0.0 58.7 %copy-start.8 = (s32[2,32]{1,0:T(2,128)S(1)}, s32[2,32]{1,0:T(2,128)}, u32[]{:S(2)}) copy-start(s32[2,32]{1,0:T(2,128)} %lp_ref.1) | copy-start | bytes 772
  0.0 58.7 %copy-start.3 = (bf16[32,64,64]{2,1,0:T(8,128)(2,1)S(1)}, bf16[32,64,64]{2,1,0:T(8,128)(2,1)}, u32[]{:S(2)}) copy-start(bf16[32,64,64]{2,1,0:T(8,128)(2,1)} %lb_ref.1) | copy-start | bytes 786436
  0.1 58.7 %copy-start.7 = (s32[2,80]{1,0:T(2,128)S(1)}, s32[2,80]{1,0:T(2,128)}, u32[]{:S(2)}) copy-start(s32[2,80]{1,0:T(2,128)} %np_ref.1) | copy-start | bytes 1924
  10.2 3.4 %copy-start = (bf16[510,64,64]{2,1,0:T(8,128)(2,1)S(1)}, bf16[510,64,64]{2,1,0:T(8,128)(2,1)}, u32[]{:S(2)}) copy-start(bf16[510,64,64]{2,1,0:T(8,128)(2,1)} %copy.12.refs_6_) | copy-start | bytes 12533764

commit v2 on v1

v2 whole, which is shorter than its diff:
```python
import jax
import jax.numpy as jnp
from jax import lax
from jax.experimental import pallas as pl
from jax.experimental.pallas import tpu as pltpu
from jax.sharding import PartitionSpec as P

LEAF = 256
MEMB = 16
ROWS = 40
C2 = 6.244106943016823
AMP = 0.0625
LN2 = 0.6931471805599453
UNROLL = 4
CUT = (32, 64)
MESH = pl.DeviceIdType.MESH
F32 = jnp.float32
BF16 = jnp.bfloat16


def dot(a, b, nt=False):
    dims = (((1,), (1,)), ((), ())) if nt else (((1,), (0,)), ((), ()))
    return lax.dot_general(a, b, dims, preferred_element_type=F32)


def split2(c):
    hi = c.astype(BF16)
    lo = (c - hi.astype(F32)).astype(BF16)
    return jnp.concatenate([hi, lo], axis=0)


def dot2(c, w, nt=False):
    n = c.shape[0]
    r = dot(split2(c), w, nt)
    return r[:n] + r[n:]


def pack(c):
    h = c.shape[0] // 2
    return jnp.concatenate([c[:h], c[h:]], axis=1)


def unpack(p):
    h = p.shape[1] // 2
    return jnp.concatenate([p[:, :h], p[:, h:]], axis=0)


def split3(x):
    a = x.astype(BF16).astype(F32)
    y = x - a
    b = y.astype(BF16).astype(F32)
    return a, b, (y - b).astype(BF16).astype(F32)


def features(xyz):
    x, y, z = xyz[0:1], xyz[1:2], xyz[2:3]
    norm = C2 * (x * x + y * y + z * z)
    n = split3(norm)
    m = [split3(-2.0 * C2 * v) for v in (x, y, z)]
    one = jnp.ones_like(x)
    zero = jnp.zeros_like(x)
    tgt = [x, y, z] * 3 + list(n) + [one] * 3 + [zero]
    src = [m[c][part] for part in range(3) for c in range(3)] + [one] * 3 + list(n) + [zero]
    row = lax.broadcasted_iota(jnp.int32, (16, xyz.shape[1]), 0)

    def build(rows):
        out = jnp.zeros((16, xyz.shape[1]), F32)
        for i, v in enumerate(rows[:15]):
            out = jnp.where(row == i, v, out)
        return out.astype(BF16)

    return build(tgt), build(src)


def up_levels(leaves, values, weights):
    out = list(values)
    start, breadth = 0, leaves
    while breadth > 1:
        for i in range(breadth // 2):
            left, right = start + 2 * i, start + 2 * i + 1
            out.append(dot2(out[left], weights(left)) + dot2(out[right], weights(right)))
        start += breadth
        breadth //= 2
    return out


def kernel(
    groups,
    coords_ref,
    rhs_ref,
    basis_ref,
    lt_ref,
    lb_ref,
    upairs_ref,
    ub_ref,
    npv_ref,
    lpv_ref,
    np_ref,
    lp_ref,
    nc_ref,
    ut_ref,
    out_ref,
    utv_ref,
    ege_ref,
    eg_ref,
    meta_ref,
    smeta_ref,
    lowwin_ref,
    fswin_ref,
    rhswin_ref,
    ftl_ref,
    fst_ref,
    rw_ref,
    inc_ref,
    lowbuf_ref,
    req_ref,
    tab_ref,
    send2_ref,
    recv2_ref,
    s_ref,
    pr_ref,
    send3_ref,
    recv3_ref,
    tabd_ref,
    send4_ref,
    recv4_ref,
    oh3_ref,
    loc_sem,
    halo_s,
    halo_r,
    req_s,
    req_r,
    p1_s,
    p1_r,
    p2_s,
    p2_r,
    p3_s,
    p3_r,
    p4_s,
    p4_r,
):
    ndev = groups * MEMB
    depth = ndev.bit_length() - 1
    subs = lax.axis_size("sub")
    dev = lax.axis_index("grp") * subs + lax.axis_index("sub")
    g = dev // MEMB
    m = dev % MEMB
    leaves = rhs_ref.shape[1] // LEAF
    low_count = 2 * leaves - 2
    near_cap = npv_ref.shape[1]
    low_dev = lpv_ref.shape[1]

    def at_dev(d):
        return (d // subs, d % subs)

    def other_group(i):
        return ((g + i) % groups) * MEMB + m

    def other_member(i):
        return g * MEMB + (m + i) % MEMB

    barrier = pltpu.get_barrier_semaphore()

    def greet(to):
        def body(i, c):
            pl.semaphore_signal(barrier, inc=1, device_id=at_dev(to(i)), device_id_type=MESH)
            return c

        return body

    after, before = (dev + 1) % ndev, (dev + ndev - 1) % ndev
    lax.fori_loop(1, groups, greet(other_group), 0)
    lax.fori_loop(1, MEMB, greet(other_member), 0)
    for d in (after, before):
        pl.semaphore_signal(barrier, inc=1, device_id=at_dev(d), device_id_type=MESH)

    get_ut = pltpu.make_async_copy(ut_ref, utv_ref, loc_sem.at[0])
    get_ut.start()

    def start(copy, count):
        def body(i, c):
            copy(i).start()
            return c

        lax.fori_loop(1, count, body, 0)

    def await_recv(copy, count):
        def body(i, c):
            copy(i).wait_recv()
            return c

        lax.fori_loop(1, count, body, 0)

    def await_send(copy, count):
        def body(i, c):
            copy(i).wait_send()
            return c

        lax.fori_loop(1, count, body, 0)

    def remote(src, dst, send, recv, to):
        return pltpu.make_async_remote_copy(src, dst, send, recv, device_id=at_dev(to), device_id_type=MESH)

    srow = lax.broadcasted_iota(jnp.int32, (8, 128), 0)
    slane = lax.broadcasted_iota(jnp.int32, (8, 128), 1)
    tile = jnp.zeros((8, 128), jnp.int32)
    for i in range(8):
        tile = jnp.where(srow == i, jnp.where(slane < 64, upairs_ref[1, i], upairs_ref[0, i]), tile)
    req_ref[g] = tile

    first = [
        dot(rhs_ref[:, l * LEAF : (l + 1) * LEAF], basis_ref[:, l * LEAF : (l + 1) * LEAF], nt=True)
        for l in range(leaves)
    ]
    low = up_levels(leaves, first, lambda i: lt_ref[i])
    tab_ref[MEMB * 16 :, :] = jnp.zeros(((ROWS - MEMB) * 16, 128), F32)
    mine = pl.ds(pl.multiple_of(m * 16, 16), 16)
    tab_ref[mine, :] = pack(low[-1])
    for i in range(low_count):
        lowwin_ref[low_count + i] = pack(low[i])
    ft, fs = features(coords_ref[...].astype(F32))
    fswin_ref[1] = fs
    for l in range(leaves):
        ftl_ref[l] = ft[:, l * LEAF : (l + 1) * LEAF]

    pl.semaphore_wait(barrier, groups - 1 + MEMB - 1 + 2)

    def copy1(i):
        return remote(tab_ref.at[mine], tab_ref.at[mine], p1_s.at[i], p1_r.at[i], other_member(i))

    def copy_req(i):
        return remote(req_ref.at[g], req_ref.at[g], req_s.at[i], req_r.at[i], other_group(i))

    start(copy1, MEMB)
    start(copy_req, groups)
    halo = []
    for side, to in ((0, after), (1, before)):
        for j, (src, dst) in enumerate((
            (fswin_ref.at[1], fswin_ref.at[2 * side]),
            (rhs_ref, rhswin_ref.at[2 * side]),
            (lowwin_ref.at[pl.ds(low_count, low_count)], lowwin_ref.at[pl.ds(2 * side * low_count, low_count)]),
        )):
            k = j * 2 + side
            halo.append(remote(src, dst, halo_s.at[k], halo_r.at[k], to))
    for c in halo:
        c.start()

    def chain(pairs, live, first_target, targets):
        n = pairs.shape[1]
        t = pairs[0:1, :] - first_target
        t = jnp.concatenate([t, jnp.full((1, 128 - n), -1, jnp.int32)], axis=1)
        down = jnp.transpose(jnp.broadcast_to(t, (128, 128)))
        slot = lax.broadcasted_iota(jnp.int32, (128, 128), 0)
        lane = lax.broadcasted_iota(jnp.int32, (128, 128), 1)
        ok = slot < live
        prev = jnp.max(jnp.where(ok & (slot < lane) & (down == t), slot + 1, 0), axis=0, keepdims=True)
        last = jnp.max(jnp.where(ok & (down == lane) & (lane < targets), slot + 1, 0), axis=0, keepdims=True)
        return prev, last

    rows = chain(npv_ref[...], nc_ref[0], dev * leaves, leaves) + chain(lpv_ref[...], low_dev, dev * low_count, low_count)
    meta_ref[...] = jnp.concatenate(list(rows) + [jnp.zeros((4, 128), jnp.int32)], axis=0)
    to_scalar = pltpu.make_async_copy(meta_ref, smeta_ref, loc_sem.at[1])
    to_scalar.start()

    def row_ids(trow):
        ids = jnp.full(trow.shape, -1, jnp.int32)
        row = 0
        for level in range(depth):
            base = 2 * ndev - 2 * (ndev >> level)
            count = max(1, MEMB >> level)
            at = base + (g * count if level <= 4 else g // (1 << (level - 4)))
            ids = jnp.where((trow >= row) & (trow < row + count), at + trow - row, ids)
            row += count
        return ids

    clusters = ut_ref.shape[2]
    pick = lax.broadcasted_iota(jnp.int32, (ROWS, clusters), 1) == row_ids(
        lax.broadcasted_iota(jnp.int32, (ROWS, clusters), 0)
    )
    pick = jnp.where(pick, 1.0, 0.0).astype(BF16)
    get_ut.wait()
    for i in range(32):
        x = jnp.concatenate([utv_ref[i], utv_ref[i + 32]], axis=0)
        ege_ref[i * ROWS : (i + 1) * ROWS, :] = dot(pick, x, nt=True)
    used = 2 * MEMB - 1 + depth - 5
    for c in range(used):
        eg_ref[c] = unpack(ege_ref[pl.ds(c, 32, stride=ROWS), :]).astype(BF16)

    await_recv(copy_req, groups)
    lane = lax.broadcasted_iota(jnp.int32, (1, 2 * ROWS), 1)
    half = lane // ROWS
    cid = row_ids(lane % ROWS)

    def onehot(column):
        pieces = []
        for other in range(groups):
            eq = (column[other] == cid).astype(F32)
            for part in range(2):
                pieces.append(jnp.where(half == part, eq, 0.0))
        return jnp.concatenate(pieces, axis=0)

    req = req_ref[...]
    oh2 = onehot([req[o][:, 0:1] for o in range(groups)]).astype(BF16)
    oh3_ref[...] = jnp.transpose(onehot([req[o][:, 64:65] for o in range(groups)])).astype(BF16)

    await_recv(copy1, MEMB)

    roots = [unpack(tab_ref[i * 16 : (i + 1) * 16, :]) for i in range(MEMB)]
    table = up_levels(MEMB, roots, lambda i: eg_ref[i])
    for level in range(5, depth):
        table.append(dot2(table[-1], eg_ref[len(table) - 1]))
    for i in range(MEMB, len(table)):
        tab_ref[i * 16 : (i + 1) * 16, :] = pack(table[i])

    for vq in range(8):
        t = jnp.concatenate([tab_ref[pl.ds(vs * 8 + vq, ROWS, stride=16), :] for vs in range(2)], axis=0)
        out = dot(oh2, t.astype(BF16)).astype(BF16)
        send2_ref[:, vq * 16 : (vq + 1) * 16, :] = out.reshape(groups, 16, 128)
    recv2_ref[g] = send2_ref[g]

    def copy2(i):
        return remote(send2_ref.at[(g + i) % groups], recv2_ref.at[g], p2_s.at[i], p2_r.at[i], other_group(i))

    start(copy2, groups)

    to_scalar.wait()
    for c in halo:
        c.wait_recv()
    inc_ref[0] = jnp.zeros(inc_ref.shape[1:], F32)
    for w in range(3):
        for l in range(leaves):
            cols = slice(l * LEAF, (l + 1) * LEAF)
            fst_ref[w * leaves + l] = jnp.transpose(fswin_ref[w, :, cols].astype(F32)).astype(BF16)
            rw_ref[w * leaves + l] = rhs_ref[:, cols] if w == 1 else rhswin_ref[w, :, cols]

    def near(lo, hi):
        def body(b, c):
            made = []
            for u in range(UNROLL):
                k = b * UNROLL + u
                t = jnp.clip(np_ref[0, k] - dev * leaves, 0, leaves - 1)
                s = jnp.clip(np_ref[1, k] - (dev - 1) * leaves, 0, 3 * leaves - 1)
                sq = jnp.maximum(dot(fst_ref[s], ftl_ref[t]), 1e-30)
                p = sq * lax.rsqrt(sq)
                tile = ((AMP + (AMP * LN2) * p) * jnp.exp2(-p)).astype(BF16)
                made.append(dot(rw_ref[s], tile))
            for u in range(UNROLL):
                k = b * UNROLL + u
                inc_ref[k + 1] = made[u] + inc_ref[smeta_ref[0, k]]
            return c

        lax.fori_loop(lo // UNROLL, hi // UNROLL, body, 0)

    near(0, CUT[0])
    await_recv(copy2, groups)
    total = recv2_ref[0].astype(F32)
    for o in range(1, groups):
        total = total + recv2_ref[o].astype(F32)
    s_ref[...] = total

    for i in range(8):
        x = jnp.concatenate([s_ref[pl.ds(vs * 8 + i, 8, stride=16), :] for vs in range(2)], axis=0)
        pr_ref[i * 16 : (i + 1) * 16, :] = pack(dot2(unpack(x), ub_ref[i], nt=True))
    send3_ref[...] = jnp.concatenate(
        [pr_ref[pl.ds(vs * 8 + vq, 8, stride=16), :] for vq in range(8) for vs in range(2)], axis=0
    ).astype(BF16)
    recv3_ref[g] = send3_ref[...]

    def copy3(i):
        return remote(send3_ref, recv3_ref.at[g], p3_s.at[i], p3_r.at[i], other_group(i))

    start(copy3, groups)
    near(CUT[0], CUT[1])
    await_recv(copy3, groups)

    oh3 = oh3_ref[...]
    for vq in range(8):
        r = recv3_ref[:, vq * 16 : (vq + 1) * 16, :].reshape(groups * 16, 128)
        tabd_ref[vq * 2 * ROWS : (vq + 1) * 2 * ROWS, :] = dot(oh3, r)

    def summed(c):
        return unpack(
            jnp.concatenate([tabd_ref[pl.ds(vs * ROWS + c, 8, stride=2 * ROWS), :] for vs in range(2)], axis=0)
        )

    at = len(table) - 1
    down = summed(at)
    while at > 2 * MEMB - 2:
        at -= 1
        down = summed(at) + dot2(down, eg_ref[at], nt=True)
    current = [down]
    breadth = 2
    while breadth <= MEMB:
        at = 2 * MEMB - 2 * breadth
        current = [summed(at + i) + dot2(current[i // 2], eg_ref[at + i], nt=True) for i in range(breadth)]
        breadth *= 2
    for i in range(MEMB):
        send4_ref[i] = pack(current[i])
    recv4_ref[m] = send4_ref[m]

    def copy4(i):
        return remote(send4_ref.at[(m + i) % MEMB], recv4_ref.at[m], p4_s.at[i], p4_r.at[i], other_member(i))

    start(copy4, MEMB)

    lowbuf_ref[0] = jnp.zeros(lowbuf_ref.shape[1:], F32)
    made = []
    for k in range(low_dev):
        s = jnp.clip(lp_ref[1, k] - (dev - 1) * low_count, 0, 3 * low_count - 1)
        made.append(dot2(unpack(lowwin_ref[s]), lb_ref[k], nt=True))
    for k in range(low_dev):
        lowbuf_ref[k + 1] = made[k] + lowbuf_ref[smeta_ref[2, k]]
    near(CUT[1], near_cap)

    await_recv(copy4, MEMB)
    total = recv4_ref[0]
    for i in range(1, MEMB):
        total = total + recv4_ref[i]
    current = [unpack(total)]
    breadth = 2
    while breadth <= leaves:
        at = 2 * leaves - 2 * breadth
        current = [
            lowbuf_ref[smeta_ref[3, at + i]] + dot2(current[i // 2], lt_ref[at + i], nt=True) for i in range(breadth)
        ]
        breadth *= 2
    for l in range(leaves):
        cols = slice(l * LEAF, (l + 1) * LEAF)
        out_ref[:, cols] = inc_ref[smeta_ref[1, l]] + dot2(current[l], basis_ref[:, cols])

    for c in halo:
        c.wait_send()
    await_send(copy_req, groups)
    await_send(copy1, MEMB)
    await_send(copy2, groups)
    await_send(copy3, groups)
    await_send(copy4, MEMB)


def on_device(coords, rhs, basis, lt, lp, lb, ut, up, ub, npairs, ncount):
    ndev = lax.axis_size(("grp", "sub"))
    groups = ndev // MEMB
    points = rhs.shape[1]
    leaves = points // LEAF
    low_count = 2 * leaves - 2
    near_cap = npairs.shape[1]
    vm = pl.BlockSpec(memory_space=pltpu.VMEM)
    sm = pl.BlockSpec(memory_space=pltpu.SMEM)
    dma = pltpu.SemaphoreType.DMA
    ut = jnp.transpose(ut, (1, 2, 0))
    return pl.pallas_call(
        lambda *refs: kernel(groups, *refs),
        out_shape=jax.ShapeDtypeStruct((32, points), F32),
        in_specs=[vm, vm, vm, vm, vm, sm, vm, vm, vm, sm, sm, sm, pl.BlockSpec(memory_space=pl.ANY)],
        out_specs=vm,
        scratch_shapes=[
            pltpu.VMEM(ut.shape, BF16),
            pltpu.VMEM((32 * ROWS, 128), F32),
            pltpu.VMEM((ROWS, 64, 64), BF16),
            pltpu.VMEM((8, 128), jnp.int32),
            pltpu.SMEM((8, 128), jnp.int32),
            pltpu.VMEM((3 * low_count, 16, 128), F32),
            pltpu.VMEM((3, 16, points), BF16),
            pltpu.VMEM((3, 32, points), BF16),
            pltpu.VMEM((leaves, 16, LEAF), BF16),
            pltpu.VMEM((3 * leaves, LEAF, 16), BF16),
            pltpu.VMEM((3 * leaves, 32, LEAF), BF16),
            pltpu.VMEM((near_cap + 1, 32, LEAF), F32),
            pltpu.VMEM((lp.shape[1] + 1, 32, 64), F32),
            pltpu.VMEM((groups, 8, 128), jnp.int32),
            pltpu.VMEM((ROWS * 16, 128), F32),
            pltpu.VMEM((groups, 128, 128), BF16),
            pltpu.VMEM((groups, 128, 128), BF16),
            pltpu.VMEM((128, 128), F32),
            pltpu.VMEM((128, 128), F32),
            pltpu.VMEM((128, 128), BF16),
            pltpu.VMEM((groups, 128, 128), BF16),
            pltpu.VMEM((8 * 2 * ROWS, 128), F32),
            pltpu.VMEM((MEMB, 16, 128), F32),
            pltpu.VMEM((MEMB, 16, 128), F32),
            pltpu.VMEM((2 * ROWS, groups * 16), BF16),
            dma((2,)),
            dma((6,)),
            dma((6,)),
            dma((groups,)),
            dma((groups,)),
            dma((MEMB,)),
            dma((MEMB,)),
            dma((groups,)),
            dma((groups,)),
            dma((groups,)),
            dma((groups,)),
            dma((MEMB,)),
            dma((MEMB,)),
        ],
        compiler_params=pltpu.CompilerParams(
            collective_id=0, has_side_effects=True, vmem_limit_bytes=56 * 2**20
        ),
        name="tree_product",
    )(coords, rhs, basis, lt, lb, up, ub, npairs, lp, npairs, lp, ncount, ut)


def solution(mesh):
    both = ("grp", "sub")
    in_specs = (
        P(None, both), P(None, both), P(None, both), P(both), P(None, both), P(both),
        P(), P(None, both), P(both), P(None, both), P(both),
    )
    return jax.shard_map(on_device, mesh=mesh, in_specs=in_specs, out_specs=P(None, both), check_vma=False)
```

time: 85.4 us -> 51.1 us (0.60)
  the two profiles are of different devices: /device:TPU:3 before, /device:TPU:1 now
where the time goes in v2:
time: 51.1 us; the launch traced here: 50.9 us
  Pallas kernels  48.6 us (95%)
  local copies, waits for them, and re-layouts  1.67 us (3%)
  between operations  0.66 us (1%)
    pallas_call x1, Pallas kernels, on_device(): pl.pallas_call(lambda *refs: kernel(groups, *refs), out_shape=jax.ShapeDt...  48.6 us
    unnamed x1, local copies, waits for them, and re-layouts  1.67 us

profile of v2, /device:TPU:1, one launch (start us, length us, event | category | flops | bytes accessed | tf_op | source)
XLA Modules:
  0.0 50.9 jit_solution(11940202248333662593)
XLA Ops:
  0.7 48.6 %tree_product.1 = f32[32,2048]{1,0:T(8,128)} custom-call(bf16[3,2048]{1,0:T(4,128)(2,1)} %refs_0_.1, bf16[32,2048]{1,0:T(8,128)(2,1)} %refs_1_.1, bf16[64,2048]{1,0:T(8,128)(2,1)} %refs_2_.1, bf16[14,64,64]{2,1,0:T(8,128)(2,1)} %refs_3_.1, bf16[32,64,64]{2,1,0:T(8,128)(2,1)} %refs_4_.1, s32[2,8]{1,0:T(2,128)} %refs_5_.1, bf16[8,64,64]{2,1,0:T(8,128)(2,1)} %refs_6_.1, ...), custom_call_target="tpu_custom_call" | custom-call | tf_op jit(solution)/shard_map/tree_product/pallas_call | solution.py:451
  49.3 1.7 %copy.14 = f32[32,2048]{1,0:T(8,128)} copy(f32[32,2048]{1,0:T(8,128)} %tree_product.1) | data formatting | bytes 524288

commit v3 on v2

--- a/solution.py
+++ b/solution.py
@@ -12,7 +12,7 @@
 AMP = 0.0625
 LN2 = 0.6931471805599453
 UNROLL = 4
-CUT = (32, 64)
+CUT = (24, 60)
 MESH = pl.DeviceIdType.MESH
 F32 = jnp.float32
 BF16 = jnp.bfloat16
@@ -90,9 +90,9 @@
     rhs_ref,
     basis_ref,
     lt_ref,
-    lb_ref,
+    lbh_ref,
     upairs_ref,
-    ub_ref,
+    ubh_ref,
     npv_ref,
     lpv_ref,
     np_ref,
@@ -101,6 +101,8 @@
     ut_ref,
     out_ref,
     utv_ref,
+    lb_ref,
+    ub_ref,
     ege_ref,
     eg_ref,
     meta_ref,
@@ -175,7 +177,11 @@
         pl.semaphore_signal(barrier, inc=1, device_id=at_dev(d), device_id_type=MESH)
 
     get_ut = pltpu.make_async_copy(ut_ref, utv_ref, loc_sem.at[0])
+    get_ub = pltpu.make_async_copy(ubh_ref, ub_ref, loc_sem.at[2])
+    get_lb = pltpu.make_async_copy(lbh_ref, lb_ref, loc_sem.at[3])
     get_ut.start()
+    get_ub.start()
+    get_lb.start()
 
     def start(copy, count):
         def body(i, c):
@@ -242,8 +248,6 @@
         )):
             k = j * 2 + side
             halo.append(remote(src, dst, halo_s.at[k], halo_r.at[k], to))
-    for c in halo:
-        c.start()
 
     def chain(pairs, live, first_target, targets):
         n = pairs.shape[1]
@@ -279,6 +283,8 @@
     )
     pick = jnp.where(pick, 1.0, 0.0).astype(BF16)
     get_ut.wait()
+    get_ub.wait()
+    get_lb.wait()
     for i in range(32):
         x = jnp.concatenate([utv_ref[i], utv_ref[i + 32]], axis=0)
         ege_ref[i * ROWS : (i + 1) * ROWS, :] = dot(pick, x, nt=True)
@@ -304,6 +310,8 @@
     oh3_ref[...] = jnp.transpose(onehot([req[o][:, 64:65] for o in range(groups)])).astype(BF16)
 
     await_recv(copy1, MEMB)
+    for c in halo:
+        c.start()
 
     roots = [unpack(tab_ref[i * 16 : (i + 1) * 16, :]) for i in range(MEMB)]
     table = up_levels(MEMB, roots, lambda i: eg_ref[i])
@@ -446,15 +454,18 @@
     near_cap = npairs.shape[1]
     vm = pl.BlockSpec(memory_space=pltpu.VMEM)
     sm = pl.BlockSpec(memory_space=pltpu.SMEM)
+    anym = pl.BlockSpec(memory_space=pl.ANY)
     dma = pltpu.SemaphoreType.DMA
     ut = jnp.transpose(ut, (1, 2, 0))
     return pl.pallas_call(
         lambda *refs: kernel(groups, *refs),
         out_shape=jax.ShapeDtypeStruct((32, points), F32),
-        in_specs=[vm, vm, vm, vm, vm, sm, vm, vm, vm, sm, sm, sm, pl.BlockSpec(memory_space=pl.ANY)],
+        in_specs=[vm, vm, vm, vm, anym, sm, anym, vm, vm, sm, sm, sm, anym],
         out_specs=vm,
         scratch_shapes=[
             pltpu.VMEM(ut.shape, BF16),
+            pltpu.VMEM(lb.shape, BF16),
+            pltpu.VMEM(ub.shape, BF16),
             pltpu.VMEM((32 * ROWS, 128), F32),
             pltpu.VMEM((ROWS, 64, 64), BF16),
             pltpu.VMEM((8, 128), jnp.int32),
@@ -479,7 +490,7 @@
             pltpu.VMEM((MEMB, 16, 128), F32),
             pltpu.VMEM((MEMB, 16, 128), F32),
             pltpu.VMEM((2 * ROWS, groups * 16), BF16),
-            dma((2,)),
+            dma((4,)),
             dma((6,)),
             dma((6,)),
             dma((groups,)),

time: 51.1 us -> 50.7 us (level)
  no operation moved by 1% of the time
where the time goes in v3:
time: 50.7 us; the launch traced here: 50.6 us
  Pallas kernels  48.2 us (95%)
  local copies, waits for them, and re-layouts  1.67 us (3%)
  between operations  0.66 us (1%)
    pallas_call x1, Pallas kernels, on_device(): pl.pallas_call(lambda *refs: kernel(groups, *refs), out_shape=jax.ShapeDt...  48.2 us
    unnamed x1, local copies, waits for them, and re-layouts  1.67 us

profile of v3, /device:TPU:1, one launch (start us, length us, event | category | flops | bytes accessed | tf_op | source)
XLA Modules:
  0.0 50.6 jit_solution(6476744586262657411)
XLA Ops:
  0.7 48.2 %tree_product.1 = f32[32,2048]{1,0:T(8,128)} custom-call(bf16[3,2048]{1,0:T(4,128)(2,1)} %refs_0_.1, bf16[32,2048]{1,0:T(8,128)(2,1)} %refs_1_.1, bf16[64,2048]{1,0:T(8,128)(2,1)} %refs_2_.1, bf16[14,64,64]{2,1,0:T(8,128)(2,1)} %refs_3_.1, bf16[32,64,64]{2,1,0:T(8,128)(2,1)} %refs_4_.1, s32[2,8]{1,0:T(2,128)} %refs_5_.1, bf16[8,64,64]{2,1,0:T(8,128)(2,1)} %refs_6_.1, ...), custom_call_target="tpu_custom_call" | custom-call | tf_op jit(solution)/shard_map/tree_product/pallas_call | solution.py:460
  48.9 1.7 %copy.14 = f32[32,2048]{1,0:T(8,128)} copy(f32[32,2048]{1,0:T(8,128)} %tree_product.1) | data formatting | bytes 524288

commit v4 on v2

--- a/solution.py
+++ b/solution.py
@@ -11,8 +11,8 @@
 C2 = 6.244106943016823
 AMP = 0.0625
 LN2 = 0.6931471805599453
-UNROLL = 4
-CUT = (32, 64)
+UNROLL = 8
+CUT = (24, 24, 56, 56)
 MESH = pl.DeviceIdType.MESH
 F32 = jnp.float32
 BF16 = jnp.bfloat16
@@ -86,21 +86,31 @@
 
 def kernel(
     groups,
-    coords_ref,
+    coords_hbm,
+    rhs_hbm,
+    basis_hbm,
+    lt_hbm,
+    up_hbm,
+    np_hbm,
+    lp_hbm,
+    nc_hbm,
+    ut_hbm,
+    ub_hbm,
+    lb_hbm,
+    out_ref,
     rhs_ref,
     basis_ref,
     lt_ref,
-    lb_ref,
-    upairs_ref,
-    ub_ref,
+    coords_ref,
+    up_ref,
     npv_ref,
     lpv_ref,
+    nc_ref,
     np_ref,
     lp_ref,
-    nc_ref,
-    ut_ref,
-    out_ref,
     utv_ref,
+    ub_ref,
+    lb_ref,
     ege_ref,
     eg_ref,
     meta_ref,
@@ -114,6 +124,7 @@
     inc_ref,
     lowbuf_ref,
     req_ref,
+    root_ref,
     tab_ref,
     send2_ref,
     recv2_ref,
@@ -145,7 +156,7 @@
     dev = lax.axis_index("grp") * subs + lax.axis_index("sub")
     g = dev // MEMB
     m = dev % MEMB
-    leaves = rhs_ref.shape[1] // LEAF
+    leaves = rhs_hbm.shape[1] // LEAF
     low_count = 2 * leaves - 2
     near_cap = npv_ref.shape[1]
     low_dev = lpv_ref.shape[1]
@@ -159,7 +170,27 @@
     def other_member(i):
         return g * MEMB + (m + i) % MEMB
 
+    fetched = []
+    for j, (src, dst) in enumerate((
+        (rhs_hbm, rhs_ref),
+        (basis_hbm, basis_ref),
+        (lt_hbm, lt_ref),
+        (up_hbm, up_ref),
+        (coords_hbm, coords_ref),
+        (np_hbm, npv_ref),
+        (lp_hbm, lpv_ref),
+        (nc_hbm, nc_ref),
+        (np_hbm, np_ref),
+        (lp_hbm, lp_ref),
+        (ut_hbm, utv_ref),
+        (ub_hbm, ub_ref),
+        (lb_hbm, lb_ref),
+    )):
+        fetched.append(pltpu.make_async_copy(src, dst, loc_sem.at[j + 1]))
+        fetched[-1].start()
+
     barrier = pltpu.get_barrier_semaphore()
+
 
     def greet(to):
         def body(i, c):
@@ -174,9 +205,6 @@
     for d in (after, before):
         pl.semaphore_signal(barrier, inc=1, device_id=at_dev(d), device_id_type=MESH)
 
-    get_ut = pltpu.make_async_copy(ut_ref, utv_ref, loc_sem.at[0])
-    get_ut.start()
-
     def start(copy, count):
         def body(i, c):
             copy(i).start()
@@ -201,38 +229,43 @@
     def remote(src, dst, send, recv, to):
         return pltpu.make_async_remote_copy(src, dst, send, recv, device_id=at_dev(to), device_id_type=MESH)
 
-    srow = lax.broadcasted_iota(jnp.int32, (8, 128), 0)
-    slane = lax.broadcasted_iota(jnp.int32, (8, 128), 1)
-    tile = jnp.zeros((8, 128), jnp.int32)
-    for i in range(8):
-        tile = jnp.where(srow == i, jnp.where(slane < 64, upairs_ref[1, i], upairs_ref[0, i]), tile)
-    req_ref[g] = tile
-
+    for c in fetched[:3]:
+        c.wait()
     first = [
         dot(rhs_ref[:, l * LEAF : (l + 1) * LEAF], basis_ref[:, l * LEAF : (l + 1) * LEAF], nt=True)
         for l in range(leaves)
     ]
     low = up_levels(leaves, first, lambda i: lt_ref[i])
-    tab_ref[MEMB * 16 :, :] = jnp.zeros(((ROWS - MEMB) * 16, 128), F32)
-    mine = pl.ds(pl.multiple_of(m * 16, 16), 16)
-    tab_ref[mine, :] = pack(low[-1])
+    root_ref[m] = pack(low[-1]).astype(BF16)
+
+    def column(row):
+        wide = jnp.concatenate([row, jnp.full((1, 128 - row.shape[1]), -1, jnp.int32)], axis=1)
+        return wide, jnp.transpose(jnp.broadcast_to(wide, (128, 128)))
+
+    fetched[3].wait()
+    slane = lax.broadcasted_iota(jnp.int32, (8, 128), 1)
+    req_ref[g] = jnp.where(slane < 64, column(up_ref[1:2, :])[1][:8], column(up_ref[0:1, :])[1][:8])
+
+    pl.semaphore_wait(barrier, groups - 1 + MEMB - 1 + 2)
+
+    def copy1(i):
+        return remote(root_ref.at[m], root_ref.at[m], p1_s.at[i], p1_r.at[i], other_member(i))
+
+    def copy_req(i):
+        return remote(req_ref.at[g], req_ref.at[g], req_s.at[i], req_r.at[i], other_group(i))
+
+    start(copy1, MEMB)
+    start(copy_req, groups)
+
+    tab_ref[:, MEMB * 8 :, :] = jnp.zeros((2, (ROWS - MEMB) * 8, 128), F32)
     for i in range(low_count):
         lowwin_ref[low_count + i] = pack(low[i])
+    for c in fetched[4:8]:
+        c.wait()
     ft, fs = features(coords_ref[...].astype(F32))
     fswin_ref[1] = fs
     for l in range(leaves):
         ftl_ref[l] = ft[:, l * LEAF : (l + 1) * LEAF]
-
-    pl.semaphore_wait(barrier, groups - 1 + MEMB - 1 + 2)
-
-    def copy1(i):
-        return remote(tab_ref.at[mine], tab_ref.at[mine], p1_s.at[i], p1_r.at[i], other_member(i))
-
-    def copy_req(i):
-        return remote(req_ref.at[g], req_ref.at[g], req_s.at[i], req_r.at[i], other_group(i))
-
-    start(copy1, MEMB)
-    start(copy_req, groups)
     halo = []
     for side, to in ((0, after), (1, before)):
         for j, (src, dst) in enumerate((
@@ -242,14 +275,9 @@
         )):
             k = j * 2 + side
             halo.append(remote(src, dst, halo_s.at[k], halo_r.at[k], to))
-    for c in halo:
-        c.start()
 
     def chain(pairs, live, first_target, targets):
-        n = pairs.shape[1]
-        t = pairs[0:1, :] - first_target
-        t = jnp.concatenate([t, jnp.full((1, 128 - n), -1, jnp.int32)], axis=1)
-        down = jnp.transpose(jnp.broadcast_to(t, (128, 128)))
+        t, down = column(pairs[0:1, :] - first_target)
         slot = lax.broadcasted_iota(jnp.int32, (128, 128), 0)
         lane = lax.broadcasted_iota(jnp.int32, (128, 128), 1)
         ok = slot < live
@@ -257,9 +285,9 @@
         last = jnp.max(jnp.where(ok & (down == lane) & (lane < targets), slot + 1, 0), axis=0, keepdims=True)
         return prev, last
 
-    rows = chain(npv_ref[...], nc_ref[0], dev * leaves, leaves) + chain(lpv_ref[...], low_dev, dev * low_count, low_count)
+    rows = chain(npv_ref[...], nc_ref[...], dev * leaves, leaves) + chain(lpv_ref[...], low_dev, dev * low_count, low_count)
     meta_ref[...] = jnp.concatenate(list(rows) + [jnp.zeros((4, 128), jnp.int32)], axis=0)
-    to_scalar = pltpu.make_async_copy(meta_ref, smeta_ref, loc_sem.at[1])
+    to_scalar = pltpu.make_async_copy(meta_ref, smeta_ref, loc_sem.at[0])
     to_scalar.start()
 
     def row_ids(trow):
@@ -273,12 +301,13 @@
             row += count
         return ids
 
-    clusters = ut_ref.shape[2]
+    clusters = utv_ref.shape[2]
     pick = lax.broadcasted_iota(jnp.int32, (ROWS, clusters), 1) == row_ids(
         lax.broadcasted_iota(jnp.int32, (ROWS, clusters), 0)
     )
     pick = jnp.where(pick, 1.0, 0.0).astype(BF16)
-    get_ut.wait()
+    for c in fetched[8:]:
+        c.wait()
     for i in range(32):
         x = jnp.concatenate([utv_ref[i], utv_ref[i + 32]], axis=0)
         ege_ref[i * ROWS : (i + 1) * ROWS, :] = dot(pick, x, nt=True)
@@ -303,25 +332,37 @@
     oh2 = onehot([req[o][:, 0:1] for o in range(groups)]).astype(BF16)
     oh3_ref[...] = jnp.transpose(onehot([req[o][:, 64:65] for o in range(groups)])).astype(BF16)
 
+    def copy2(h):
+        def copy(i):
+            part = pl.ds(h * 64, 64)
+            return remote(
+                send2_ref.at[(g + i) % groups, part], recv2_ref.at[g, part], p2_s.at[h, i], p2_r.at[h, i], other_group(i)
+            )
+
+        return copy
+
+    def climb(h):
+        roots = [root_ref[i].astype(F32)[h * 8 : h * 8 + 8] for i in range(MEMB)]
+        for i in range(MEMB):
+            tab_ref[h, i * 8 : i * 8 + 8, :] = roots[i]
+        table = up_levels(MEMB, [unpack(r) for r in roots], lambda i: eg_ref[i])
+        for level in range(5, depth):
+            table.append(dot2(table[-1], eg_ref[len(table) - 1]))
+        for i in range(MEMB, len(table)):
+            tab_ref[h, i * 8 : i * 8 + 8, :] = pack(table[i])
+        for b in range(h * 4, h * 4 + 4):
+            t = jnp.concatenate([tab_ref[h, pl.ds(2 * b + vs - 8 * h, ROWS, stride=8), :] for vs in range(2)], axis=0)
+            out = dot(oh2, t.astype(BF16)).astype(BF16)
+            send2_ref[:, b * 16 : (b + 1) * 16, :] = out.reshape(groups, 16, 128)
+        part = pl.ds(h * 64, 64)
+        recv2_ref[g, part] = send2_ref[g, part]
+        start(copy2(h), groups)
+
+    for c in halo:
+        c.start()
     await_recv(copy1, MEMB)
-
-    roots = [unpack(tab_ref[i * 16 : (i + 1) * 16, :]) for i in range(MEMB)]
-    table = up_levels(MEMB, roots, lambda i: eg_ref[i])
-    for level in range(5, depth):
-        table.append(dot2(table[-1], eg_ref[len(table) - 1]))
-    for i in range(MEMB, len(table)):
-        tab_ref[i * 16 : (i + 1) * 16, :] = pack(table[i])
-
-    for vq in range(8):
-        t = jnp.concatenate([tab_ref[pl.ds(vs * 8 + vq, ROWS, stride=16), :] for vs in range(2)], axis=0)
-        out = dot(oh2, t.astype(BF16)).astype(BF16)
-        send2_ref[:, vq * 16 : (vq + 1) * 16, :] = out.reshape(groups, 16, 128)
-    recv2_ref[g] = send2_ref[g]
-
-    def copy2(i):
-        return remote(send2_ref.at[(g + i) % groups], recv2_ref.at[g], p2_s.at[i], p2_r.at[i], other_group(i))
-
-    start(copy2, groups)
+    climb(0)
+    climb(1)
 
     to_scalar.wait()
     for c in halo:
@@ -351,57 +392,98 @@
 
         lax.fori_loop(lo // UNROLL, hi // UNROLL, body, 0)
 
+    def copy3(h):
+        def copy(i):
+            part = pl.ds(h * 64, 64)
+            return remote(send3_ref.at[part], recv3_ref.at[g, part], p3_s.at[h, i], p3_r.at[h, i], other_group(i))
+
+        return copy
+
+    def couple(h):
+        part = pl.ds(h * 64, 64)
+        total = recv2_ref[0, part].astype(F32)
+        for o in range(1, groups):
+            total = total + recv2_ref[o, part].astype(F32)
+        s_ref[part, :] = total
+        for i in range(8):
+            x = s_ref[pl.ds(h * 64 + i, 8, stride=8), :]
+            pr_ref[h * 64 + i * 8 : h * 64 + i * 8 + 8, :] = pack(dot2(unpack(x), ub_ref[i], nt=True))
+        made = jnp.concatenate([pr_ref[pl.ds(h * 64 + v, 8, stride=8), :] for v in range(8)], axis=0).astype(BF16)
+        send3_ref[part, :] = made
+        recv3_ref[g, part] = made
+        start(copy3(h), groups)
+
+    def copy4(h):
+        def copy(i):
+            part = pl.ds(h * 8, 8)
+            return remote(
+                send4_ref.at[(m + i) % MEMB, part], recv4_ref.at[m, part], p4_s.at[h, i], p4_r.at[h, i], other_member(i)
+            )
+
+        return copy
+
+    def descend(h):
+        oh3 = oh3_ref[...]
+        for b in range(h * 4, h * 4 + 4):
+            r = recv3_ref[:, b * 16 : (b + 1) * 16, :].reshape(groups * 16, 128)
+            tabd_ref[b * 2 * ROWS : (b + 1) * 2 * ROWS, :] = dot(oh3, r)
+
+        def summed(c):
+            return unpack(tabd_ref[pl.ds(h * 8 * ROWS + c, 8, stride=ROWS), :])
+
+        at = used - 1
+        down = summed(at)
+        while at > 2 * MEMB - 2:
+            at -= 1
+            down = summed(at) + dot2(down, eg_ref[at], nt=True)
+        current = [down]
+        breadth = 2
+        while breadth <= MEMB:
+            at = 2 * MEMB - 2 * breadth
+            current = [summed(at + i) + dot2(current[i // 2], eg_ref[at + i], nt=True) for i in range(breadth)]
+            breadth *= 2
+        for i in range(MEMB):
+            send4_ref[i, h * 8 : h * 8 + 8] = pack(current[i])
+        part = pl.ds(h * 8, 8)
+        recv4_ref[m, part] = send4_ref[m, part]
+        start(copy4(h), MEMB)
+
+    def finish(h):
+        part = pl.ds(h * 8, 8)
+        total = recv4_ref[0, part]
+        for i in range(1, MEMB):
+            total = total + recv4_ref[i, part]
+        current = [unpack(total)]
+        lower, upper = slice(h * 8, h * 8 + 8), slice(16 + h * 8, 24 + h * 8)
+        breadth = 2
+        while breadth <= leaves:
+            at = 2 * leaves - 2 * breadth
+            grown = []
+            for i in range(breadth):
+                last = smeta_ref[3, at + i]
+                own = jnp.concatenate([lowbuf_ref[last, lower], lowbuf_ref[last, upper]], axis=0)
+                grown.append(own + dot2(current[i // 2], lt_ref[at + i], nt=True))
+            current = grown
+            breadth *= 2
+        for l in range(leaves):
+            cols = slice(l * LEAF, (l + 1) * LEAF)
+            far = dot2(current[l], basis_ref[:, cols])
+            last = smeta_ref[1, l]
+            out_ref[lower, cols] = inc_ref[last, lower] + far[:8]
+            out_ref[upper, cols] = inc_ref[last, upper] + far[8:]
+
     near(0, CUT[0])
-    await_recv(copy2, groups)
-    total = recv2_ref[0].astype(F32)
-    for o in range(1, groups):
-        total = total + recv2_ref[o].astype(F32)
-    s_ref[...] = total
-
-    for i in range(8):
-        x = jnp.concatenate([s_ref[pl.ds(vs * 8 + i, 8, stride=16), :] for vs in range(2)], axis=0)
-        pr_ref[i * 16 : (i + 1) * 16, :] = pack(dot2(unpack(x), ub_ref[i], nt=True))
-    send3_ref[...] = jnp.concatenate(
-        [pr_ref[pl.ds(vs * 8 + vq, 8, stride=16), :] for vq in range(8) for vs in range(2)], axis=0
-    ).astype(BF16)
-    recv3_ref[g] = send3_ref[...]
-
-    def copy3(i):
-        return remote(send3_ref, recv3_ref.at[g], p3_s.at[i], p3_r.at[i], other_group(i))
-
-    start(copy3, groups)
+    await_recv(copy2(0), groups)
+    couple(0)
     near(CUT[0], CUT[1])
-    await_recv(copy3, groups)
-
-    oh3 = oh3_ref[...]
-    for vq in range(8):
-        r = recv3_ref[:, vq * 16 : (vq + 1) * 16, :].reshape(groups * 16, 128)
-        tabd_ref[vq * 2 * ROWS : (vq + 1) * 2 * ROWS, :] = dot(oh3, r)
-
-    def summed(c):
-        return unpack(
-            jnp.concatenate([tabd_ref[pl.ds(vs * ROWS + c, 8, stride=2 * ROWS), :] for vs in range(2)], axis=0)
-        )
-
-    at = len(table) - 1
-    down = summed(at)
-    while at > 2 * MEMB - 2:
-        at -= 1
-        down = summed(at) + dot2(down, eg_ref[at], nt=True)
-    current = [down]
-    breadth = 2
-    while breadth <= MEMB:
-        at = 2 * MEMB - 2 * breadth
-        current = [summed(at + i) + dot2(current[i // 2], eg_ref[at + i], nt=True) for i in range(breadth)]
-        breadth *= 2
-    for i in range(MEMB):
-        send4_ref[i] = pack(current[i])
-    recv4_ref[m] = send4_ref[m]
-
-    def copy4(i):
-        return remote(send4_ref.at[(m + i) % MEMB], recv4_ref.at[m], p4_s.at[i], p4_r.at[i], other_member(i))
-
-    start(copy4, MEMB)
+    await_recv(copy2(1), groups)
+    couple(1)
+    near(CUT[1], CUT[2])
+    await_recv(copy3(0), groups)
+    descend(0)
+    near(CUT[2], CUT[3])
+    await_recv(copy3(1), groups)
+    descend(1)
 
     lowbuf_ref[0] = jnp.zeros(lowbuf_ref.shape[1:], F32)
     made = []
@@ -410,31 +492,19 @@
         made.append(dot2(unpack(lowwin_ref[s]), lb_ref[k], nt=True))
     for k in range(low_dev):
         lowbuf_ref[k + 1] = made[k] + lowbuf_ref[smeta_ref[2, k]]
-    near(CUT[1], near_cap)
-
-    await_recv(copy4, MEMB)
-    total = recv4_ref[0]
-    for i in range(1, MEMB):
-        total = total + recv4_ref[i]
-    current = [unpack(total)]
-    breadth = 2
-    while breadth <= leaves:
-        at = 2 * leaves - 2 * breadth
-        current = [
-            lowbuf_ref[smeta_ref[3, at + i]] + dot2(current[i // 2], lt_ref[at + i], nt=True) for i in range(breadth)
-        ]
-        breadth *= 2
-    for l in range(leaves):
-        cols = slice(l * LEAF, (l + 1) * LEAF)
-        out_ref[:, cols] = inc_ref[smeta_ref[1, l]] + dot2(current[l], basis_ref[:, cols])
-
+    near(CUT[3], near_cap)
+
+    for h in range(2):
+        await_recv(copy4(h), MEMB)
+        finish(h)
     for c in halo:
         c.wait_send()
     await_send(copy_req, groups)
     await_send(copy1, MEMB)
-    await_send(copy2, groups)
-    await_send(copy3, groups)
-    await_send(copy4, MEMB)
+    for h in range(2):
+        await_send(copy2(h), groups)
+        await_send(copy3(h), groups)
+        await_send(copy4(h), MEMB)
 
 
 def on_device(coords, rhs, basis, lt, lp, lb, ut, up, ub, npairs, ncount):
@@ -445,16 +515,28 @@
     low_count = 2 * leaves - 2
     near_cap = npairs.shape[1]
     vm = pl.BlockSpec(memory_space=pltpu.VMEM)
-    sm = pl.BlockSpec(memory_space=pltpu.SMEM)
+    anym = pl.BlockSpec(memory_space=pl.ANY)
     dma = pltpu.SemaphoreType.DMA
     ut = jnp.transpose(ut, (1, 2, 0))
     return pl.pallas_call(
         lambda *refs: kernel(groups, *refs),
         out_shape=jax.ShapeDtypeStruct((32, points), F32),
-        in_specs=[vm, vm, vm, vm, vm, sm, vm, vm, vm, sm, sm, sm, pl.BlockSpec(memory_space=pl.ANY)],
+        in_specs=[anym] * 11,
         out_specs=vm,
         scratch_shapes=[
+            pltpu.VMEM(rhs.shape, BF16),
+            pltpu.VMEM(basis.shape, BF16),
+            pltpu.VMEM(lt.shape, BF16),
+            pltpu.VMEM(coords.shape, BF16),
+            pltpu.VMEM(up.shape, jnp.int32),
+            pltpu.VMEM(npairs.shape, jnp.int32),
+            pltpu.VMEM(lp.shape, jnp.int32),
+            pltpu.VMEM((1, 1), jnp.int32),
+            pltpu.SMEM(npairs.shape, jnp.int32),
+            pltpu.SMEM(lp.shape, jnp.int32),
             pltpu.VMEM(ut.shape, BF16),
+            pltpu.VMEM(ub.shape, BF16),
+            pltpu.VMEM(lb.shape, BF16),
             pltpu.VMEM((32 * ROWS, 128), F32),
             pltpu.VMEM((ROWS, 64, 64), BF16),
             pltpu.VMEM((8, 128), jnp.int32),
@@ -468,7 +550,8 @@
             pltpu.VMEM((near_cap + 1, 32, LEAF), F32),
             pltpu.VMEM((lp.shape[1] + 1, 32, 64), F32),
             pltpu.VMEM((groups, 8, 128), jnp.int32),
-            pltpu.VMEM((ROWS * 16, 128), F32),
+            pltpu.VMEM((MEMB, 16, 128), BF16),
+            pltpu.VMEM((2, ROWS * 8, 128), F32),
             pltpu.VMEM((groups, 128, 128), BF16),
             pltpu.VMEM((groups, 128, 128), BF16),
             pltpu.VMEM((128, 128), F32),
@@ -479,25 +562,25 @@
             pltpu.VMEM((MEMB, 16, 128), F32),
             pltpu.VMEM((MEMB, 16, 128), F32),
             pltpu.VMEM((2 * ROWS, groups * 16), BF16),
-            dma((2,)),
+            dma((14,)),
             dma((6,)),
             dma((6,)),
             dma((groups,)),
             dma((groups,)),
             dma((MEMB,)),
             dma((MEMB,)),
-            dma((groups,)),
-            dma((groups,)),
-            dma((groups,)),
-            dma((groups,)),
-            dma((MEMB,)),
-            dma((MEMB,)),
+            dma((2, groups)),
+            dma((2, groups)),
+            dma((2, groups)),
+            dma((2, groups)),
+            dma((2, MEMB)),
+            dma((2, MEMB)),
         ],
         compiler_params=pltpu.CompilerParams(
             collective_id=0, has_side_effects=True, vmem_limit_bytes=56 * 2**20
         ),
         name="tree_product",
-    )(coords, rhs, basis, lt, lb, up, ub, npairs, lp, npairs, lp, ncount, ut)
+    )(coords, rhs, basis, lt, up, npairs, lp, ncount.reshape(1, 1), ut, ub, lb)
 
 
 def solution(mesh):

time: 51.1 us -> 48.1 us (0.941)
  Pallas kernels: 48.6 us -> 45.7 us
    pallas_call x1, Pallas kernels: 48.6 us -> 45.7 us  [on_device(): pl.pallas_call(lambda *refs: kernel(groups, *refs), out_shape=jax.ShapeDt...]
where the time goes in v4:
time: 48.1 us; the launch traced here: 48 us
  Pallas kernels  45.7 us (95%)
  local copies, waits for them, and re-layouts  1.67 us (3%)
  between operations  0.66 us (1%)
    pallas_call x1, Pallas kernels, on_device(): pl.pallas_call(lambda *refs: kernel(groups, *refs), out_shape=jax.ShapeDt...  45.7 us
    unnamed x1, local copies, waits for them, and re-layouts  1.67 us

profile of v4, /device:TPU:1, one launch (start us, length us, event | category | flops | bytes accessed | tf_op | source)
XLA Modules:
  0.0 48.0 jit_solution(15010714064856390764)
XLA Ops:
  0.7 45.7 %tree_product.1 = f32[32,2048]{1,0:T(8,128)} custom-call(bf16[3,2048]{1,0:T(4,128)(2,1)} %refs_0_.1, bf16[32,2048]{1,0:T(8,128)(2,1)} %refs_1_.1, bf16[64,2048]{1,0:T(8,128)(2,1)} %refs_2_.1, bf16[14,64,64]{2,1,0:T(8,128)(2,1)} %refs_3_.1, s32[2,8]{1,0:T(2,128)} %refs_4_.1, s32[2,80]{1,0:T(2,128)} %refs_5_.1, s32[2,32]{1,0:T(2,128)} %refs_6_.1, ...), custom_call_target="tpu_custom_call" | custom-call | tf_op jit(solution)/shard_map/tree_product/pallas_call | solution.py:521
  46.3 1.7 %copy.14 = f32[32,2048]{1,0:T(8,128)} copy(f32[32,2048]{1,0:T(8,128)} %tree_product.1) | data formatting | bytes 524288

commit v5 on v4

--- a/solution.py
+++ b/solution.py
@@ -276,6 +276,9 @@
             k = j * 2 + side
             halo.append(remote(src, dst, halo_s.at[k], halo_r.at[k], to))
 
+    for c in halo:
+        c.start()
+
     def chain(pairs, live, first_target, targets):
         t, down = column(pairs[0:1, :] - first_target)
         slot = lax.broadcasted_iota(jnp.int32, (128, 128), 0)
@@ -358,8 +361,6 @@
         recv2_ref[g, part] = send2_ref[g, part]
         start(copy2(h), groups)
 
-    for c in halo:
-        c.start()
     await_recv(copy1, MEMB)
     climb(0)
     climb(1)

time: 48.1 us -> 47 us (0.977)
  Pallas kernels: 45.7 us -> 44.5 us
    pallas_call x1, Pallas kernels: 45.7 us -> 44.5 us  [on_device(): pl.pallas_call(lambda *refs: kernel(groups, *refs), out_shape=jax.ShapeDt...]
where the time goes in v5:
time: 47 us; the launch traced here: 46.9 us
  Pallas kernels  44.5 us (95%)
  local copies, waits for them, and re-layouts  1.67 us (4%)
  between operations  0.66 us (1%)
    pallas_call x1, Pallas kernels, on_device(): pl.pallas_call(lambda *refs: kernel(groups, *refs), out_shape=jax.ShapeDt...  44.5 us
    unnamed x1, local copies, waits for them, and re-layouts  1.67 us

profile of v5, /device:TPU:1, one launch (start us, length us, event | category | flops | bytes accessed | tf_op | source)
XLA Modules:
  0.0 46.9 jit_solution(32842216834302649)
XLA Ops:
  0.7 44.5 %tree_product.1 = f32[32,2048]{1,0:T(8,128)} custom-call(bf16[3,2048]{1,0:T(4,128)(2,1)} %refs_0_.1, bf16[32,2048]{1,0:T(8,128)(2,1)} %refs_1_.1, bf16[64,2048]{1,0:T(8,128)(2,1)} %refs_2_.1, bf16[14,64,64]{2,1,0:T(8,128)(2,1)} %refs_3_.1, s32[2,8]{1,0:T(2,128)} %refs_4_.1, s32[2,80]{1,0:T(2,128)} %refs_5_.1, s32[2,32]{1,0:T(2,128)} %refs_6_.1, ...), custom_call_target="tpu_custom_call" | custom-call | tf_op jit(solution)/shard_map/tree_product/pallas_call | solution.py:522
  45.2 1.7 %copy.14 = f32[32,2048]{1,0:T(8,128)} copy(f32[32,2048]{1,0:T(8,128)} %tree_product.1) | data formatting | bytes 524288

commit v6 on v5

--- a/solution.py
+++ b/solution.py
@@ -11,8 +11,8 @@
 C2 = 6.244106943016823
 AMP = 0.0625
 LN2 = 0.6931471805599453
-UNROLL = 8
-CUT = (24, 24, 56, 56)
+UNROLL = 16
+CUT = (32, 32, 64, 64)
 MESH = pl.DeviceIdType.MESH
 F32 = jnp.float32
 BF16 = jnp.bfloat16

time: 47 us -> 47.9 us (1.019)
  Pallas kernels: 44.5 us -> 45.4 us
    pallas_call x1, Pallas kernels: 44.5 us -> 45.4 us  [on_device(): pl.pallas_call(lambda *refs: kernel(groups, *refs), out_shape=jax.ShapeDt...]
where the time goes in v6:
time: 47.9 us; the launch traced here: 47.8 us
  Pallas kernels  45.4 us (95%)
  local copies, waits for them, and re-layouts  1.67 us (3%)
  between operations  0.66 us (1%)
    pallas_call x1, Pallas kernels, on_device(): pl.pallas_call(lambda *refs: kernel(groups, *refs), out_shape=jax.ShapeDt...  45.4 us
    unnamed x1, local copies, waits for them, and re-layouts  1.67 us

profile of v6, /device:TPU:1, one launch (start us, length us, event | category | flops | bytes accessed | tf_op | source)
XLA Modules:
  0.0 47.8 jit_solution(13854125066947056838)
XLA Ops:
  0.7 45.4 %tree_product.1 = f32[32,2048]{1,0:T(8,128)} custom-call(bf16[3,2048]{1,0:T(4,128)(2,1)} %refs_0_.1, bf16[32,2048]{1,0:T(8,128)(2,1)} %refs_1_.1, bf16[64,2048]{1,0:T(8,128)(2,1)} %refs_2_.1, bf16[14,64,64]{2,1,0:T(8,128)(2,1)} %refs_3_.1, s32[2,8]{1,0:T(2,128)} %refs_4_.1, s32[2,80]{1,0:T(2,128)} %refs_5_.1, s32[2,32]{1,0:T(2,128)} %refs_6_.1, ...), custom_call_target="tpu_custom_call" | custom-call | tf_op jit(solution)/shard_map/tree_product/pallas_call | solution.py:522
  46.1 1.7 %copy.14 = f32[32,2048]{1,0:T(8,128)} copy(f32[32,2048]{1,0:T(8,128)} %tree_product.1) | data formatting | bytes 524288
